TPU v7x, 256 devices: a whole 4x4x8 slice. The times are simulated.
256 devices in a mesh: grp: 8 (over z_hi, core), wide: 32 (over z_lo, y, x).
Axes of the slice: x: 4, y: 4, z: 8 (z_hi: 4, z_lo: 2; z = z_hi * 2 + z_lo), core: 2. Of those that a mesh axis runs over, the one named last changes fastest.
Arguments:
- echoes: bfloat16 [2, 128, 2048, 1024], P(None, 'wide', None, 'grp'), may hold values from -6 to 6
- patterns: bfloat16 [256, 2, 64], replicated, may hold values from -0.125 to 0.125
- block_choice: int32 [512, 16], replicated, may hold values from 0 to 255
Outputs:
- beams: bfloat16 [512, 2, 2048, 128], P('grp', None, 'wide')
Inputs may be any that keep to these rules, and one draw needn't show every extreme that they name: `block_choice`: each entry names one of the 256 block patterns.
All inputs are finite; a program needn't handle non-finite values.
Results may differ from a plain program's by a relative error of at most 0.0065.
Values may be sent and summed in bfloat16 or wider, within the bound.
A program may use at most 128 MiB of HBM per device.

v0:
```python
import math

import jax
import jax.numpy as jnp
from jax import lax
from jax.sharding import PartitionSpec as P


def doppler_matrix(length):
    bin_index = jnp.arange(length, dtype=jnp.int32)
    phases = bin_index[:, None] * bin_index[None, :] % length
    angles = phases.astype(jnp.float32) * (2.0 * math.pi / length)
    scale_factor = 1.0 / math.sqrt(length)
    cosine = (jnp.cos(angles) * scale_factor).astype(jnp.bfloat16)
    sine_part = (-jnp.sin(angles) * scale_factor).astype(jnp.bfloat16)
    upper_rows = jnp.stack([cosine, -sine_part], axis=1)
    lower_rows = jnp.stack([sine_part, cosine], axis=1)
    return jnp.stack([upper_rows, lower_rows], axis=0)


def steering(patterns, block_choice):
    pattern_count = patterns.shape[0]
    one_hot = (
        block_choice[:, :, None] == jnp.arange(pattern_count, dtype=jnp.int32)[None, None, :]
    ).astype(jnp.bfloat16)
    picked = jnp.einsum(
        "bjq,qot->bojt", one_hot, patterns, preferred_element_type=jnp.float32
    ).astype(jnp.bfloat16)
    flattened = picked.reshape(picked.shape[0], 2, -1)
    real_part = flattened[:, 0]
    imag_part = flattened[:, 1]
    upper_rows = jnp.stack([real_part, -imag_part], axis=1)
    lower_rows = jnp.stack([imag_part, real_part], axis=1)
    return jnp.stack([upper_rows, lower_rows], axis=1)


def form_beams(arrived, dft_table, grouped):
    group_count = grouped.shape[3]
    gate_count = arrived.shape[4]
    samples = arrived.reshape(2, arrived.shape[1], gate_count, group_count, -1)
    doppler = jnp.einsum(
        "okip,ipngc->gocnk", dft_table, samples, preferred_element_type=jnp.float32
    ).astype(jnp.bfloat16)
    partials = jnp.einsum(
        "boigc,gicnk->gbonk", grouped, doppler, preferred_element_type=jnp.float32
    )
    rounded = lax.optimization_barrier(partials.astype(jnp.bfloat16)).astype(jnp.float32)
    return jnp.sum(rounded, axis=0).astype(jnp.bfloat16)


def send_home(local_beams):
    return lax.all_to_all(local_beams, "grp", split_axis=0, concat_axis=2, tiled=True)


def shards(echoes, patterns, block_choice):
    wide_count = lax.axis_size("wide")
    group_count = lax.axis_size("grp")
    local_pulses = echoes.shape[1]
    all_gates = echoes.shape[2]
    chan_local = echoes.shape[3]
    pulse_count = local_pulses * wide_count
    gates_dev = all_gates // wide_count
    sub_gates = gates_dev // group_count
    dft_table = doppler_matrix(pulse_count)
    weights = steering(patterns, block_choice)
    beam_count = weights.shape[0]
    grouped = weights.reshape(beam_count, 2, 2, group_count, chan_local)
    shaped = echoes.reshape(2, local_pulses, wide_count, group_count, sub_gates, chan_local)
    turned = lax.all_to_all(
        lax.all_to_all(shaped, "grp", split_axis=3, concat_axis=5, tiled=True),
        "wide",
        split_axis=2,
        concat_axis=1,
        tiled=True,
    )
    local_beams = form_beams(turned, dft_table, grouped)
    return send_home(local_beams)


def solution(mesh):
    placed = (P(None, "wide", None, "grp"), P(), P())
    return jax.shard_map(
        shards, mesh=mesh, in_specs=placed, out_specs=P("grp", None, "wide", None), check_vma=False
    )
```

profile of v0, /device:TPU:8, one launch (start us, length us, event | category | flops | bytes accessed | tf_op | source)
XLA Modules:
  0.0 273.9 jit_solution(5966931205546747388)
XLA Ops:
  0.0 0.0 copy-start
  0.0 3.4 %copy.37 = bf16[2,4,32,8,8,128]{5,4,2,1,0,3:T(8,128)(2,1)S(1)} copy(bf16[2,4,32,8,8,128]{5,4,3,2,1,0:T(8,128)(2,1)} %bitcast.75) | data formatting | bytes 8388608 | tf_op jit(solution)/shard_map/reshape | solution.py:68
  3.4 105.3 %all_to_all.51 = bf16[2,4,32,8,8,128]{5,4,2,1,0,3:T(8,128)(2,1)S(1)} all-to-all(bf16[2,4,32,8,8,128]{5,4,2,1,0,3:T(8,128)(2,1)S(1)} %copy.37), channel_id=1, replica_groups=mesh['grp'=8,'wide'=32] {'grp'}, dimensions={3} | all-to-all | bytes 8388608 | tf_op jit(solution)/shard_map/all_to_all | solution.py:70
  108.7 6.8 %copy.51 = bf16[2,4,32,1,8,8,128]{6,5,4,1,0,2,3:T(8,128)(2,1)} copy(bf16[2,4,32,1,8,8,128]{6,4,2,1,0,5,3:T(8,128)(2,1)S(1)} %bitcast.69) | data formatting | bytes 8388608 | tf_op jit(solution)/shard_map/all_to_all | solution.py:70
  115.5 7.3 %reshape.117 = bf16[2,4,32,1,8,1024]{5,4,1,0,3,2:T(8,128)(2,1)} reshape(bf16[2,4,32,1,8,8,128]{6,5,4,1,0,2,3:T(8,128)(2,1)} %copy.51) | data formatting | bytes 8388608 | tf_op jit(solution)/shard_map/all_to_all | solution.py:70
  122.8 7.7 %all-to-all-start.1 = ((bf16[2,4,32,1,8,1024]{5,4,1,0,3,2:T(8,128)(2,1)}), bf16[2,4,32,1,8,1024]{5,4,1,0,3,2:T(8,128)(2,1)}, u32[]{:S(2)}, u32[]{:S(2)}) async-start(bf16[2,4,32,1,8,1024]{5,4,1,0,3,2:T(8,128)(2,1)} %reshape.117), calls=%async_computation.1 | async-start | bytes 8388608 | tf_op jit(solution)/shard_map/all_to_all | solution.py:69
  130.6 2.5 convert_bitcast_fusion
  133.1 0.2 copy.34
  133.3 0.2 slice_negate_fusion
  133.5 1.7 pad_maximum_fusion
  135.2 3.9 %copy.35 = bf16[512,1,2,8,128]{4,0,2,1,3:T(8,128)(2,1)} copy(bf16[512,1,2,8,128]{0,4,3,2,1:T(8,128)(2,1)} %bitcast.72) | data formatting | bytes 4194304 | tf_op jit(solution)/shard_map/stack | solution.py:34
  139.1 2.4 copy.36
  141.5 0.3 fusion.21
  141.7 0.3 multiply_convert_fusion
  142.0 40.2 %all-to-all-done.1 = bf16[2,4,32,1,8,1024]{5,4,1,0,3,2:T(8,128)(2,1)} async-done(((bf16[2,4,32,1,8,1024]{5,4,1,0,3,2:T(8,128)(2,1)}), bf16[2,4,32,1,8,1024]{5,4,1,0,3,2:T(8,128)(2,1)}, u32[]{:S(2)}, u32[]{:S(2)}) %all-to-all-start.1) | async-done | bytes 4194336 | tf_op jit(solution)/shard_map/all_to_all | solution.py:69
  182.2 2.6 copy.40
  184.9 1.1 copy.57
  186.0 7.4 %fusion.7 = bf16[2,128,8,8,128,1]{4,1,5,0,2,3:T(8,128)(2,1)} fusion(bf16[2,128,8,8,128,1]{4,3,2,1,0,5:T(8,128)(2,1)S(1)} %bitcast.68, bf16[1,128,2,128]{3,1,2,0:T(8,128)(2,1)S(1)} %get-tuple-element.11, bf16[1,128,2,128]{3,1,2,0:T(8,128)(2,1)S(1)} %get-tuple-element.10), kind=kOutput, calls=%fused_computation.9 | convolution fusion | flops 1074003968 | bytes 8519680 | tf_op jit(solution)/shard_map/okip,ipngc->gocnk/dot_general | solution.py:41
  193.4 10.6 %bitcast_convert_fusion = bf16[8,512,2,8,128]{4,1,3,2,0:T(8,128)(2,1)} fusion(bf16[2,128,8,8,128,1]{4,1,5,0,2,3:T(8,128)(2,1)} %fusion.7, bf16[512,1,2,8,128]{4,0,2,1,3:T(8,128)(2,1)} %copy.36, bf16[512,1,2,8,128]{4,0,2,1,3:T(8,128)(2,1)S(1)} %copy-done.2), kind=kOutput, calls=%fused_computation | convolution fusion | flops 4311744512 | bytes 25165824 | tf_op jit(solution)/shard_map/boigc,gicnk->gbonk/dot_general | solution.py:44
  204.0 9.4 %reduce_sum.12 = bf16[512,2,8,128]{3,0,2,1:T(8,128)(2,1)S(1)} reduce(bf16[8,512,2,8,128]{4,1,3,2,0:T(8,128)(2,1)} %bitcast_convert_fusion, bf16[]{:T(256)} %constant.21.clone.1), dimensions={0}, to_apply=%region_0.1 | reduce | flops 7340032 | bytes 18874370 | tf_op jit(solution)/shard_map/reduce_sum | solution.py:48
  213.4 0.0 copy-start.1
  213.4 1.4 copy.43
  214.8 57.2 %all_to_all.52 = bf16[512,2,8,128]{3,2,1,0:T(8,128)(2,1)S(1)} all-to-all(bf16[512,2,8,128]{3,2,1,0:T(8,128)(2,1)S(1)} %copy.43), channel_id=1, replica_groups=mesh['grp'=8,'wide'=32] {'grp'}, dimensions={0} | all-to-all | bytes 4194304 | tf_op jit(solution)/shard_map/all_to_all | solution.py:52
  272.0 1.9 copy.61
  (7 shorter events, 0.0 us)
Async XLA Ops:
  0.0 130.6 %copy-start = (bf16[256,2,64]{0,2,1:T(8,128)(2,1)S(1)}, bf16[256,2,64]{0,2,1:T(8,128)(2,1)}, u32[]{:S(2)}) copy-start(bf16[256,2,64]{0,2,1:T(8,128)(2,1)} %param.4) | copy-start | bytes 196612
  122.8 7.8 %copy-start.3 = (s32[512,16]{0,1:T(8,128)S(1)}, s32[512,16]{0,1:T(8,128)}, u32[]{:S(2)}) copy-start(s32[512,16]{0,1:T(8,128)} %param.5) | copy-start | bytes 98308
  122.8 59.4 %all-to-all-start.1 = ((bf16[2,4,32,1,8,1024]{5,4,1,0,3,2:T(8,128)(2,1)}), bf16[2,4,32,1,8,1024]{5,4,1,0,3,2:T(8,128)(2,1)}, u32[]{:S(2)}, u32[]{:S(2)}) async-start(bf16[2,4,32,1,8,1024]{5,4,1,0,3,2:T(8,128)(2,1)} %reshape.117), calls=%async_computation.1 | async-start | bytes 8388608 | tf_op jit(solution)/shard_map/all_to_all | solution.py:69
  186.0 7.4 %copy-start.2 = (bf16[512,1,2,8,128]{4,0,2,1,3:T(8,128)(2,1)S(1)}, bf16[512,1,2,8,128]{4,0,2,1,3:T(8,128)(2,1)}, u32[]{:S(2)}) copy-start(bf16[512,1,2,8,128]{4,0,2,1,3:T(8,128)(2,1)} %copy.35) | copy-start | bytes 6291460
  213.4 60.5 %copy-start.1 = (bf16[256,2,64]{0,2,1:T(8,128)(2,1)S(1)}, bf16[256,2,64]{0,2,1:T(8,128)(2,1)}, u32[]{:S(2)}) copy-start(bf16[256,2,64]{0,2,1:T(8,128)(2,1)} %param.4) | copy-start | bytes 196612
where the time goes:
time: 275 us; the launch traced here: 274 us
  blocking collectives  163 us (59%)
  waiting for transfers between devices  40.2 us (15%)
  local copies, waits for them, and re-layouts  31 us (11%)
  matrix products  20.5 us (7%)
  other arithmetic  11.8 us (4%)
  starting transfers between devices  7.73 us (3%)
    all_to_all x1, blocking collectives, shards(): lax.all_to_all(shaped, 'grp', split_axis=3, concat_axis=5, tiled=True)  105 us
    all_to_all x1, blocking collectives, send_home(): lax.all_to_all(local_beams, 'grp', split_axis=0, concat_axis=2, tiled=True)  57.2 us
    all_to_all x1, waiting for transfers between devices, shards(): lax.all_to_all(lax.all_to_all(shaped, 'grp', split_axis=3, concat_axis=5,...  40.2 us
    all_to_all x2, local copies, waits for them, and re-layouts, shards(): lax.all_to_all(shaped, 'grp', split_axis=3, concat_axis=5, tiled=True)  14.1 us
    dot_general x1, matrix products, form_beams(): jnp.einsum('boigc,gicnk->gbonk', grouped, doppler, preferred_element_type...  10.6 us
    reduce_sum x1, other arithmetic, form_beams(): return jnp.sum(rounded, axis=0).astype(jnp.bfloat16)  9.38 us
    all_to_all x1, starting transfers between devices, shards(): lax.all_to_all(lax.all_to_all(shaped, 'grp', split_axis=3, concat_axis=5,...  7.73 us
    dot_general x1, matrix products, form_beams(): jnp.einsum('okip,ipngc->gocnk', dft_table, samples, preferred_element_typ...  7.43 us
  transfers between devices with their start and end apart: 1, of which 1 were waited for; matrix products, arithmetic and copies ran while one was open for 4% of the time, Pallas kernels for 0%

commit v1 on v0

v1 whole, which is shorter than its diff:
```python
import functools
import math

import jax
import jax.numpy as jnp
import ml_dtypes
import numpy as np
from jax import lax
from jax.experimental import pallas as pl
from jax.experimental.pallas import tpu as pltpu
from jax.sharding import PartitionSpec as P

MESH = pl.DeviceIdType.MESH
CHUNKS = 2
PAIRS = 8
STRIDE = 5


def doppler_operator(length, wide):
    index = np.arange(length, dtype=np.int32)
    phases = index[:, None] * index[None, :] % length
    angles = phases.astype(np.float32) * np.float32(2.0 * math.pi / length)
    scale = np.float32(1.0 / math.sqrt(length))
    cosine = np.cos(angles) * scale
    sine = -np.sin(angles) * scale
    table = np.array([[cosine, -sine], [sine, cosine]], np.float32)
    table = table.transpose(0, 2, 1, 3).reshape(2, length, 2, wide, length // wide)
    full = np.zeros((2, 2, length, wide, 2, length // wide, 2), np.float32)
    for gate in range(2):
        full[:, gate, :, :, :, :, gate] = table.transpose(0, 1, 3, 2, 4)
    size = 4 * length
    return full.reshape(size, size).astype(ml_dtypes.bfloat16)


def pair_order():
    order = np.zeros((256, 256), np.float32)
    for block in range(2):
        for pair in range(8):
            for row in range(8):
                for gate in range(2):
                    order[block * 128 + pair * 16 + row * 2 + gate, block * 128 + row * 16 + pair * 2 + gate] = 1
    return order.astype(ml_dtypes.bfloat16)


def kernel(
    echoes, patterns, choice, operator, order, out,
    raw, turned, held, oper, perm, pats, picks, weights, dop, mine, give, got, done,
    in_sem, send_sem, recv_sem, swap_send, swap_recv, home_send, home_recv,
):
    grp, wide = lax.axis_index("grp"), lax.axis_index("wide")
    high, core = grp // 2, grp % 2
    per = PAIRS // CHUNKS

    def at(to_wide, to_high, to_core):
        return {"grp": to_high * 2 + to_core, "wide": to_wide}

    loads = [
        pltpu.make_async_copy(a, b, in_sem.at[n])
        for n, (a, b) in enumerate(
            [(echoes, raw), (order, perm), (choice, picks), (patterns, pats), (operator, oper)]
        )
    ]
    for load in loads:
        load.start()

    barrier = pltpu.get_barrier_semaphore()

    def greet(step, carry):
        pl.semaphore_signal(
            barrier,
            inc=1,
            device_id=at((wide + step // 4) % 32, (high + step % 4) % 4, core),
            device_id_type=MESH,
        )
        return carry

    lax.fori_loop(1, 128, greet, 0)
    pl.semaphore_signal(barrier, inc=1, device_id=at(wide, high, 1 - core), device_id_type=MESH)

    loads[0].wait()
    loads[1].wait()

    def turn(block, carry):
        rows = [raw[:, pl.ds(pl.multiple_of(block * 64 + n * 16, 16), 16), :].reshape(128, 128) for n in range(4)]
        both = jnp.concatenate(
            [jnp.concatenate(rows[:2], axis=0), jnp.concatenate(rows[2:], axis=0)], axis=1
        )
        moved = jnp.dot(perm[...], both, preferred_element_type=jnp.float32).astype(jnp.bfloat16)
        for n in range(4):
            part = moved[(n % 2) * 128 : (n % 2) * 128 + 128, (n // 2) * 128 : (n // 2) * 128 + 128]
            turned[block, n] = part.reshape(PAIRS, 16, 128)
        return carry

    lax.fori_loop(0, 32, turn, 0)
    pl.semaphore_wait(barrier, 128)

    def send(chunk):
        span = pl.ds(chunk * per, per)

        def one(step, carry):
            to_wide = (wide + (step // 4) * STRIDE) % 32
            to_high = (high + step % 4) % 4
            pltpu.make_async_remote_copy(
                src_ref=turned.at[to_wide, to_high, span],
                dst_ref=held.at[high, span, wide],
                send_sem=send_sem.at[chunk],
                recv_sem=recv_sem.at[chunk],
                device_id=at(to_wide, to_high, core),
                device_id_type=MESH,
            ).start()
            return carry

        lax.fori_loop(1, 128, one, 0)
        pltpu.make_async_copy(
            turned.at[wide, high, span], held.at[high, span, wide], recv_sem.at[chunk]
        ).start()

    for chunk in range(CHUNKS):
        send(chunk)

    for load in loads[2:]:
        load.wait()
    lane = lax.broadcasted_iota(jnp.int32, (512, 128), 1)
    number = lax.broadcasted_iota(jnp.int32, (512, 256), 1)
    for h in range(4):
        found = []
        for j in range(2):
            column = h * 4 + j
            pick = jnp.where(core == 0, picks[:, column : column + 1], picks[:, column + 2 : column + 3])
            hot = (pick == number).astype(jnp.float32).astype(jnp.bfloat16)
            found.append(jnp.dot(hot, pats[...], preferred_element_type=jnp.float32))
        real = jnp.where(lane < 64, found[0], pltpu.roll(found[1], 64, 1)).astype(jnp.bfloat16)
        imag = jnp.where(lane < 64, pltpu.roll(found[0], 64, 1), found[1]).astype(jnp.bfloat16)
        left, right = slice(h * 128, h * 128 + 128), slice(512 + h * 128, 512 + h * 128 + 128)
        for beams in range(8):
            rows = slice(beams * 64, beams * 64 + 64)
            upper = slice((beams // 2) * 128, (beams // 2) * 128 + 64)
            lower = slice((beams // 2) * 128 + 64, (beams // 2) * 128 + 128)
            weights[beams % 2, upper, left] = real[rows]
            weights[beams % 2, upper, right] = -imag[rows]
            weights[beams % 2, lower, left] = imag[rows]
            weights[beams % 2, lower, right] = real[rows]

    across = (((1,), (1,)), ((), ()))

    def beams_of(owner, pair):
        total = lax.dot_general(
            weights[owner, :, :512], dop[pair, :256], across, preferred_element_type=jnp.float32
        )
        return total + lax.dot_general(
            weights[owner, :, 512:], dop[pair, 256:], across, preferred_element_type=jnp.float32
        )

    def swap(pair):
        return pltpu.make_async_remote_copy(
            src_ref=give.at[pair],
            dst_ref=got.at[pair],
            send_sem=swap_send.at[pair],
            recv_sem=swap_recv.at[pair],
            device_id=at(wide, high, 1 - core),
            device_id_type=MESH,
        )

    def first(pair, carry):
        samples = jnp.concatenate([held[h, pair].reshape(512, 128) for h in range(4)], axis=1)
        dop[pair] = jnp.dot(oper[...], samples, preferred_element_type=jnp.float32).astype(jnp.bfloat16)
        give[pair] = beams_of(1 - core, pair).astype(jnp.bfloat16)
        swap(pair).start()
        return carry

    def second(pair, carry):
        mine[...] = beams_of(core, pair)
        swap(pair).wait()
        done[pair] = (mine[...] + got[pair].astype(jnp.float32)).astype(jnp.bfloat16).reshape(4, 128, 256)
        for step in (2, 1, 3):
            to_high = (high + step) % 4
            pltpu.make_async_remote_copy(
                src_ref=done.at[pair, to_high],
                dst_ref=out.at[high, pair],
                send_sem=home_send,
                recv_sem=home_recv,
                device_id=at(wide, to_high, core),
                device_id_type=MESH,
            ).start()
        pltpu.make_async_copy(done.at[pair, high], out.at[high, pair], home_recv).start()
        return carry

    for chunk in range(CHUNKS):
        arrived = held.at[:, pl.ds(chunk * per, per)]
        pltpu.make_async_copy(arrived, arrived, recv_sem.at[chunk]).wait()
        lax.fori_loop(chunk * per, chunk * per + per, first, 0)
        lax.fori_loop(chunk * per, chunk * per + per, second, 0)

    for chunk in range(CHUNKS):
        for part in (pl.ds(0, 31), pl.ds(31, 1)):
            sent = turned.at[part, :, pl.ds(chunk * per, per)]
            if part.start:
                sent = turned.at[31, pl.ds(0, 3), pl.ds(chunk * per, per)]
            pltpu.make_async_copy(sent, sent, send_sem.at[chunk]).wait()
    sent = done.at[:, pl.ds(0, 3)]
    pltpu.make_async_copy(sent, sent, home_send).wait()
    pltpu.make_async_copy(out, out, home_recv).wait()


def shards(echoes, patterns, block_choice):
    bf16 = jnp.bfloat16
    anywhere = pl.BlockSpec(memory_space=pl.ANY)
    beams = pl.pallas_call(
        kernel,
        out_shape=jax.ShapeDtypeStruct((4, PAIRS, 128, 256), bf16),
        in_specs=[anywhere] * 5,
        out_specs=anywhere,
        scratch_shapes=[
            pltpu.VMEM((8, 2048, 128), bf16),
            pltpu.VMEM((32, 4, PAIRS, 16, 128), bf16),
            pltpu.VMEM((4, PAIRS, 32, 16, 128), bf16),
            pltpu.VMEM((512, 512), bf16),
            pltpu.VMEM((256, 256), bf16),
            pltpu.VMEM((256, 128), bf16),
            pltpu.VMEM((512, 16), jnp.int32),
            pltpu.VMEM((2, 512, 1024), bf16),
            pltpu.VMEM((PAIRS, 512, 512), bf16),
            pltpu.VMEM((512, 256), jnp.float32),
            pltpu.VMEM((PAIRS, 512, 256), bf16),
            pltpu.VMEM((PAIRS, 512, 256), bf16),
            pltpu.VMEM((PAIRS, 4, 128, 256), bf16),
            pltpu.SemaphoreType.DMA((5,)),
            pltpu.SemaphoreType.DMA((CHUNKS,)),
            pltpu.SemaphoreType.DMA((CHUNKS,)),
            pltpu.SemaphoreType.DMA((PAIRS,)),
            pltpu.SemaphoreType.DMA((PAIRS,)),
            pltpu.SemaphoreType.DMA,
            pltpu.SemaphoreType.DMA,
        ],
        compiler_params=pltpu.CompilerParams(
            collective_id=0, has_side_effects=True, vmem_limit_bytes=48 << 20
        ),
    )(
        echoes.reshape(8, 2048, 128),
        patterns.reshape(256, 128),
        block_choice,
        jnp.asarray(doppler_operator(128, 32)),
        jnp.asarray(pair_order()),
    )
    return beams.reshape(4, PAIRS, 2, 64, 2, 128).transpose(3, 2, 0, 1, 4, 5).reshape(64, 2, 64, 128)


def solution(mesh):
    placed = (P(None, "wide", None, "grp"), P(), P())
    return jax.shard_map(
        shards, mesh=mesh, in_specs=placed, out_specs=P("grp", None, "wide", None), check_vma=False
    )
```

time: 275 us -> 164 us (0.60)
  blocking collectives: 163 us -> 0 us
  Pallas kernels: 0 us -> 152 us
  waiting for transfers between devices: 40.2 us -> 0 us
  matrix products: 20.5 us -> 0 us
  local copies, waits for them, and re-layouts: 31 us -> 11.1 us
  other arithmetic: 11.8 us -> 0 us
  starting transfers between devices: 7.73 us -> 0 us
    all_to_all x2 -> x0, blocking collectives: 163 us -> none  [the longest x1 105 us: shards(): lax.all_to_all(shaped, 'grp', split_axis=3, concat_axis=5, tiled=True)]
    pallas_call x0 -> x1, Pallas kernels: none -> 152 us  [shards(): pl.pallas_call(kernel, out_shape=jax.ShapeDtypeStruct((4, PAIRS, 128, 256...]
    all_to_all x1 -> x0, waiting for transfers between devices: 40.2 us -> none  [shards(): lax.all_to_all(lax.all_to_all(shaped, 'grp', split_axis=3, concat_axis=5,...]
    dot_general x3 -> x0, matrix products: 20.5 us -> none  [the longest x1 10.6 us: form_beams(): jnp.einsum('boigc,gicnk->gbonk', grouped, doppler, preferred_element_type...]
    all_to_all x4 -> x0, local copies, waits for them, and re-layouts: 18.7 us -> none  [the longest x2 14.1 us: shards(): lax.all_to_all(shaped, 'grp', split_axis=3, concat_axis=5, tiled=True)]
    reduce_sum x1 -> x0, other arithmetic: 9.38 us -> none  [form_beams(): return jnp.sum(rounded, axis=0).astype(jnp.bfloat16)]
    all_to_all x1 -> x0, starting transfers between devices: 7.73 us -> none  [shards(): lax.all_to_all(lax.all_to_all(shaped, 'grp', split_axis=3, concat_axis=5,...]
    another operation x2 -> x0, local copies, waits for them, and re-layouts: 6.25 us -> none  [steering(): return jnp.stack([upper_rows, lower_rows], axis=1)]
  transfers between devices with their start and end apart: 1 -> 0, of which waited for: 1 -> 0; matrix products, arithmetic and copies ran while one was open for 4% -> 0% of each run, Pallas kernels for 0% -> 0%
where the time goes in v1:
time: 164 us; the launch traced here: 163 us
  Pallas kernels  152 us (93%)
  local copies, waits for them, and re-layouts  11.1 us (7%)
    pallas_call x1, Pallas kernels, shards(): pl.pallas_call(kernel, out_shape=jax.ShapeDtypeStruct((4, PAIRS, 128, 256...  152 us
    transpose x1, local copies, waits for them, and re-layouts, shards(): beams.reshape(4, PAIRS, 2, 64, 2, 128).transpose(3, 2, 0, 1, 4, 5)  5.27 us

profile of v1, /device:TPU:8, one launch (start us, length us, event | category | flops | bytes accessed | tf_op | source)
XLA Modules:
  0.0 163.0 jit_solution(11955688610399211127)
XLA Ops:
  0.0 0.9 copy.9.patterns
  1.0 0.9 copy.10.choice
  1.8 0.0 copy-start
  1.9 1.0 copy-done
  2.9 0.0 copy-start.1
  2.9 0.9 copy-done.1
  3.8 151.8 %shard_map.55 = bf16[4,8,128,256]{3,2,1,0:T(8,128)(2,1)S(1)} custom-call(bf16[8,2048,128]{2,1,0:T(8,128)(2,1)} %bitcast.7, bf16[256,128]{1,0:T(8,128)(2,1)S(1)} %copy.9.patterns, s32[512,16]{1,0:T(8,128)S(1)} %copy.10.choice, bf16[512,512]{1,0:T(8,128)(2,1)S(1)} %copy-done, bf16[256,256]{1,0:T(8,128)(2,1)S(1)} %copy-done.1), custom_call_target="tpu_custom_call" | custom-call | tf_op jit(solution)/shard_map/pallas_call | solution.py:208
  155.6 2.1 %reshape.14 = bf16[4,8,2,64,2,128]{5,4,3,2,1,0:T(2,128)(2,1)} reshape(bf16[4,8,128,256]{3,2,1,0:T(8,128)(2,1)S(1)} %shard_map.55) | data formatting | bytes 4194304 | tf_op jit(solution)/shard_map/reshape | solution.py:245
  157.7 5.3 %copy.11 = bf16[64,2,4,8,2,128]{5,4,3,2,1,0:T(2,128)(2,1)} copy(bf16[64,2,4,8,2,128]{5,4,0,1,3,2:T(2,128)(2,1)} %bitcast.6) | data formatting | bytes 4194304 | tf_op jit(solution)/shard_map/transpose | solution.py:245
Async XLA Ops:
  1.8 1.0 copy-start
  2.9 0.9 copy-start.1

commit v2 on v1

v2 whole, which is shorter than its diff:
```python
import functools
import math

import jax
import jax.numpy as jnp
import ml_dtypes
import numpy as np
from jax import lax
from jax.experimental import pallas as pl
from jax.experimental.pallas import tpu as pltpu
from jax.sharding import PartitionSpec as P

MESH = pl.DeviceIdType.MESH
CHUNKS = 4
PAIRS = 8
PER = PAIRS // CHUNKS


def doppler_operator(length, wide):
    index = np.arange(length, dtype=np.int32)
    phases = index[:, None] * index[None, :] % length
    angles = phases.astype(np.float32) * np.float32(2.0 * math.pi / length)
    scale = np.float32(1.0 / math.sqrt(length))
    cosine = np.cos(angles) * scale
    sine = -np.sin(angles) * scale
    table = np.array([[cosine, -sine], [sine, cosine]], np.float32)
    table = table.transpose(0, 2, 1, 3).reshape(2, length, 2, wide, length // wide)
    full = np.zeros((2, 2, length, wide, 2, 2, length // wide), np.float32)
    for gate in range(2):
        full[:, gate, :, :, gate] = table.transpose(0, 1, 3, 2, 4)
    size = 4 * length
    return full.reshape(size, size).astype(ml_dtypes.bfloat16)


def kernel(
    echoes, patterns, choice, operator, out,
    raw, single, turned, mid, held, oper, pats, picks, weights, dop, mine, give, got, done, homed, spread, final,
    load_sem, in_sem, z_send, z_recv, xy_send, xy_recv, swap_send, swap_recv, home_send, home_recv, out_sem,
):
    grp, wide = lax.axis_index("grp"), lax.axis_index("wide")
    high, core = grp // 2, grp % 2
    low, place = wide // 16, wide % 16
    row, column = place // 4, place % 4

    def at(to_high, to_low, to_place, to_core):
        return {"grp": to_high * 2 + to_core, "wide": to_low * 16 + to_place}

    def pulled(half):
        span = pl.ds(pl.multiple_of(half * 1024, 1024), 1024)
        return pltpu.make_async_copy(echoes.at[:, span], raw.at[:, span], load_sem.at[half])

    first_half = 1 - low
    pulled(first_half).start()
    pulled(low).start()
    loads = [
        pltpu.make_async_copy(a, b, in_sem.at[n])
        for n, (a, b) in enumerate([(choice, picks), (patterns, pats), (operator, oper)])
    ]
    for load in loads:
        load.start()

    barrier = pltpu.get_barrier_semaphore()

    def greet(device):
        pl.semaphore_signal(barrier, inc=1, device_id=device, device_id_type=MESH)

    def along_z(step):
        to = (high * 2 + low + step) % 8
        return to // 2, to % 2

    def around(step):
        return ((row + step // 4) % 4) * 4 + (column + step % 4) % 4

    for step in range(1, 8):
        to_high, to_low = along_z(step)
        greet(at(to_high, to_low, place, core))
    for step in range(1, 16):
        greet(at(high, low, around(step), core))
    greet(at(high, low, place, 1 - core))

    def turn(block, carry):
        slot = block % 2
        start = pl.multiple_of(block * 64, 64)
        single[slot] = raw[:, pl.ds(start, 64), :].astype(jnp.float32)
        for h in range(4):
            for pair in range(PAIRS):
                gate = h * 16 + pair * 2
                both = jnp.concatenate([single[slot, :, gate], single[slot, :, gate + 1]], axis=0)
                turned[block, h, pair] = both.astype(jnp.bfloat16)
        return carry

    def send_z(chunk, step):
        to_high, to_low = along_z(step)
        span = pl.ds(chunk * PER, PER)
        pltpu.make_async_remote_copy(
            src_ref=turned.at[pl.ds(to_low * 16, 16), to_high, span],
            dst_ref=mid.at[:, high, span, low],
            send_sem=z_send.at[chunk],
            recv_sem=z_recv.at[chunk],
            device_id=at(to_high, to_low, place, core),
            device_id_type=MESH,
        ).start()

    def keep_z(chunk):
        span = pl.ds(chunk * PER, PER)
        pltpu.make_async_copy(
            turned.at[pl.ds(low * 16, 16), high, span], mid.at[:, high, span, low], z_recv.at[chunk]
        ).start()

    pulled(first_half).wait()
    lax.fori_loop(first_half * 16, first_half * 16 + 16, turn, 0)
    pl.semaphore_wait(barrier, 23)
    for step in (3, 5, 1, 7):
        send_z(0, step)
    pulled(low).wait()
    lax.fori_loop(low * 16, low * 16 + 16, turn, 0)
    for step in (4, 2, 6):
        send_z(0, step)
    keep_z(0)
    for chunk in range(1, CHUNKS):
        for step in (4, 3, 5, 2, 6, 1, 7):
            send_z(chunk, step)
        keep_z(chunk)

    def send_xy(chunk):
        span = pl.ds(chunk * PER, PER)
        arrived = mid.at[:, :, span]
        pltpu.make_async_copy(arrived, arrived, z_recv.at[chunk]).wait()

        def one(step, carry):
            to = around(step)
            pltpu.make_async_remote_copy(
                src_ref=mid.at[to, :, span],
                dst_ref=held.at[:, span, :, place],
                send_sem=xy_send.at[chunk],
                recv_sem=xy_recv.at[chunk],
                device_id=at(high, low, to, core),
                device_id_type=MESH,
            ).start()
            return carry

        lax.fori_loop(1, 16, one, 0)
        pltpu.make_async_copy(
            mid.at[place, :, span], held.at[:, span, :, place], xy_recv.at[chunk]
        ).start()

    for load in loads:
        load.wait()
    lane = lax.broadcasted_iota(jnp.int32, (512, 128), 1)
    number = lax.broadcasted_iota(jnp.int32, (256, 512), 0)
    for h in range(4):
        found = []
        for j in range(2):
            n = h * 4 + j
            pick = jnp.where(core == 0, picks[n : n + 1, :], picks[n + 2 : n + 3, :])
            hot = (pick == number).astype(jnp.float32).astype(jnp.bfloat16)
            found.append(jnp.dot(pats[...], hot, preferred_element_type=jnp.float32).T)
        real = jnp.where(lane < 64, found[0], pltpu.roll(found[1], 64, 1)).astype(jnp.bfloat16)
        imag = jnp.where(lane < 64, pltpu.roll(found[0], 64, 1), found[1]).astype(jnp.bfloat16)
        left, right = slice(h * 128, h * 128 + 128), slice(512 + h * 128, 512 + h * 128 + 128)
        for beams in range(8):
            rows = slice(beams * 64, beams * 64 + 64)
            upper = slice((beams // 2) * 128, (beams // 2) * 128 + 64)
            lower = slice((beams // 2) * 128 + 64, (beams // 2) * 128 + 128)
            weights[beams % 2, upper, left] = real[rows]
            weights[beams % 2, upper, right] = -imag[rows]
            weights[beams % 2, lower, left] = imag[rows]
            weights[beams % 2, lower, right] = real[rows]

    across = (((1,), (1,)), ((), ()))

    def beams_of(owner, pair):
        total = lax.dot_general(
            weights[owner, :, :512], dop[pair, :256], across, preferred_element_type=jnp.float32
        )
        return total + lax.dot_general(
            weights[owner, :, 512:], dop[pair, 256:], across, preferred_element_type=jnp.float32
        )

    def swap(pair):
        return pltpu.make_async_remote_copy(
            src_ref=give.at[pair],
            dst_ref=got.at[pair],
            send_sem=swap_send.at[pair],
            recv_sem=swap_recv.at[pair],
            device_id=at(high, low, place, 1 - core),
            device_id_type=MESH,
        )

    def first(pair, carry):
        samples = jnp.concatenate([held[h, pair].reshape(512, 128) for h in range(4)], axis=1)
        dop[pair] = jnp.dot(oper[...], samples, preferred_element_type=jnp.float32).astype(jnp.bfloat16)
        give[pair] = beams_of(1 - core, pair).astype(jnp.bfloat16)
        swap(pair).start()
        return carry

    def work(chunk):
        span = pl.ds(chunk * PER, PER)
        arrived = held.at[:, span]
        pltpu.make_async_copy(arrived, arrived, xy_recv.at[chunk]).wait()
        start = chunk * PER

        def second(pair, carry):
            mine[...] = beams_of(core, pair)
            swap(pair).wait()
            done[pair] = (mine[...] + got[pair].astype(jnp.float32)).astype(jnp.bfloat16).reshape(4, 128, 256)
            for step in (2, 1, 3):
                to_high = (high + step) % 4
                pltpu.make_async_remote_copy(
                    src_ref=done.at[pair, to_high],
                    dst_ref=homed.at[high, pair],
                    send_sem=home_send,
                    recv_sem=home_recv.at[high, chunk],
                    device_id=at(to_high, low, place, core),
                    device_id_type=MESH,
                ).start()
            pltpu.make_async_copy(
                done.at[pair, high], homed.at[high, pair], home_recv.at[high, chunk]
            ).start()
            return carry

        lax.fori_loop(start, start + PER, first, 0)
        lax.fori_loop(start, start + PER, second, 0)

    send_xy(0)
    for chunk in range(1, CHUNKS):
        send_xy(chunk)
        work(chunk - 1)
    work(CHUNKS - 1)

    for chunk in range(CHUNKS):
        for step in range(4):
            source = (high + step) % 4
            span = pl.ds(chunk * PER, PER)
            landed = homed.at[source, span]
            pltpu.make_async_copy(landed, landed, home_recv.at[source, chunk]).wait()
            for pair in range(chunk * PER, chunk * PER + PER):
                for gate in range(2):
                    piece = homed[source, pair, :, gate * 128 : gate * 128 + 128]
                    spread[source, :, pair * 2 + gate, :] = piece.astype(jnp.float32)
            if chunk == CHUNKS - 1:
                final[source] = spread[source].astype(jnp.bfloat16)
                for part in range(2):
                    pltpu.make_async_copy(
                        final.at[source, pl.ds(part * 64, 64)],
                        out.at[:, part, pl.ds(pl.multiple_of(source * 16, 16), 16)],
                        out_sem,
                    ).start()

    for chunk in range(CHUNKS):
        span = pl.ds(chunk * PER, PER)
        for part in (pl.ds(0, 16), pl.ds(16, 8), pl.ds(24, 4)):
            sent = turned.at[part, :, span]
            pltpu.make_async_copy(sent, sent, z_send.at[chunk]).wait()
        sent = mid.at[pl.ds(0, 15), :, span]
        pltpu.make_async_copy(sent, sent, xy_send.at[chunk]).wait()
    sent = done.at[:, pl.ds(0, 3)]
    pltpu.make_async_copy(sent, sent, home_send).wait()
    pltpu.make_async_copy(out, out, out_sem).wait()


def shards(echoes, patterns, block_choice):
    bf16, f32 = jnp.bfloat16, jnp.float32
    anywhere = pl.BlockSpec(memory_space=pl.ANY)
    return pl.pallas_call(
        kernel,
        out_shape=jax.ShapeDtypeStruct((64, 2, 64, 128), bf16),
        in_specs=[anywhere] + [pl.BlockSpec(memory_space=pltpu.HBM)] * 3,
        out_specs=anywhere,
        scratch_shapes=[
            pltpu.VMEM((8, 2048, 128), bf16),
            pltpu.VMEM((2, 8, 64, 128), f32),
            pltpu.VMEM((32, 4, PAIRS, 16, 128), bf16),
            pltpu.VMEM((16, 4, PAIRS, 2, 16, 128), bf16),
            pltpu.VMEM((4, PAIRS, 2, 16, 16, 128), bf16),
            pltpu.VMEM((512, 512), bf16),
            pltpu.VMEM((128, 256), bf16),
            pltpu.VMEM((16, 512), jnp.int32),
            pltpu.VMEM((2, 512, 1024), bf16),
            pltpu.VMEM((PAIRS, 512, 512), bf16),
            pltpu.VMEM((512, 256), f32),
            pltpu.VMEM((PAIRS, 512, 256), bf16),
            pltpu.VMEM((PAIRS, 512, 256), bf16),
            pltpu.VMEM((PAIRS, 4, 128, 256), bf16),
            pltpu.VMEM((4, PAIRS, 128, 256), bf16),
            pltpu.VMEM((4, 128, 16, 128), f32),
            pltpu.VMEM((4, 128, 16, 128), bf16),
            pltpu.SemaphoreType.DMA((2,)),
            pltpu.SemaphoreType.DMA((3,)),
            pltpu.SemaphoreType.DMA((CHUNKS,)),
            pltpu.SemaphoreType.DMA((CHUNKS,)),
            pltpu.SemaphoreType.DMA((CHUNKS,)),
            pltpu.SemaphoreType.DMA((CHUNKS,)),
            pltpu.SemaphoreType.DMA((PAIRS,)),
            pltpu.SemaphoreType.DMA((PAIRS,)),
            pltpu.SemaphoreType.DMA,
            pltpu.SemaphoreType.DMA((4, CHUNKS)),
            pltpu.SemaphoreType.DMA,
        ],
        compiler_params=pltpu.CompilerParams(
            collective_id=0, has_side_effects=True, vmem_limit_bytes=48 << 20
        ),
    )(
        echoes.reshape(8, 2048, 128),
        patterns.transpose(1, 2, 0).reshape(128, 256),
        block_choice.T,
        jnp.asarray(doppler_operator(128, 32)),
    )


def solution(mesh):
    placed = (P(None, "wide", None, "grp"), P(), P())
    return jax.shard_map(
        shards, mesh=mesh, in_specs=placed, out_specs=P("grp", None, "wide", None), check_vma=False
    )
```

time: 164 us -> 153 us (0.933)
  local copies, waits for them, and re-layouts: 11.1 us -> 3.96 us
  Pallas kernels: 152 us -> 148 us
    transpose x1 -> x0, local copies, waits for them, and re-layouts: 5.27 us -> none  [shards(): beams.reshape(4, PAIRS, 2, 64, 2, 128).transpose(3, 2, 0, 1, 4, 5)]
    pallas_call x1, Pallas kernels: 152 us -> 148 us  [shards(): pl.pallas_call(kernel, out_shape=jax.ShapeDtypeStruct((64, 2, 64, 128), b...]
    reshape x2 -> x0, local copies, waits for them, and re-layouts: 3.02 us -> none  [the longest x1 2.07 us: shards(): beams.reshape(4, PAIRS, 2, 64, 2, 128).transpose(3, 2, 0, 1, 4, 5)]
    unnamed x5 -> x7, local copies, waits for them, and re-layouts: 2.83 us -> 3.96 us
where the time goes in v2:
time: 153 us; the launch traced here: 151 us
  Pallas kernels  148 us (97%)
  local copies, waits for them, and re-layouts  3.96 us (3%)
    pallas_call x1, Pallas kernels, shards(): pl.pallas_call(kernel, out_shape=jax.ShapeDtypeStruct((64, 2, 64, 128), b...  148 us
    unnamed x7, local copies, waits for them, and re-layouts  3.96 us

profile of v2, /device:TPU:8, one launch (start us, length us, event | category | flops | bytes accessed | tf_op | source)
XLA Modules:
  0.0 151.5 jit_solution(9828530541903890017)
XLA Ops:
  0.0 0.0 copy-start
  0.0 1.0 copy-done
  1.0 0.0 copy-start.1
  1.0 0.8 copy-done.1
  1.9 0.0 copy-start.2
  1.9 0.8 copy-done.2
  2.6 147.5 %shard_map.46 = bf16[64,2,64,128]{3,2,1,0:T(8,128)(2,1)S(1)} custom-call(bf16[8,2048,128]{2,1,0:T(8,128)(2,1)} %bitcast.7, bf16[128,256]{1,0:T(8,128)(2,1)S(1)} %bitcast.5, s32[16,512]{1,0:T(8,128)S(1)} %bitcast.6, bf16[512,512]{1,0:T(8,128)(2,1)S(1)} %copy-done), custom_call_target="tpu_custom_call" | custom-call | tf_op jit(solution)/shard_map/pallas_call | solution.py:265
  150.2 1.3 copy.6
Async XLA Ops:
  0.0 1.0 copy-start
  1.0 0.8 copy-start.1
  1.9 0.8 copy-start.2

commit v3 on v0

v3 whole, which is shorter than its diff:
```python
import math

import jax
import jax.numpy as jnp
import ml_dtypes
import numpy as np
from jax import lax
from jax.experimental import pallas as pl
from jax.experimental.pallas import tpu as pltpu
from jax.sharding import PartitionSpec as P

MESH = pl.DeviceIdType.MESH
CHUNKS = 4


def doppler_operator(length, wide):
    index = np.arange(length, dtype=np.int32)
    phases = index[:, None] * index[None, :] % length
    angles = phases.astype(np.float32) * np.float32(2.0 * math.pi / length)
    scale = np.float32(1.0 / math.sqrt(length))
    cosine = np.cos(angles) * scale
    sine = -np.sin(angles) * scale
    table = np.array([[cosine, -sine], [sine, cosine]], np.float32)
    table = table.transpose(0, 2, 1, 3).reshape(2, length, 2, wide, length // wide)
    full = np.zeros((2, 2, length, wide, 2, 2, length // wide), np.float32)
    for gate in range(2):
        full[:, gate, :, :, gate] = table.transpose(0, 1, 3, 2, 4)
    halves = full.reshape(4 * length, 2, 2 * length).transpose(1, 0, 2)
    return halves.astype(ml_dtypes.bfloat16)


def kernel(
    echoes, patterns, choice, operator, out,
    raw, single, turned, mid, held, oper, pats, picks, weights, dop, mine, give, got, keep, pass_on, passed, done,
    homed, spread, final,
    load_sem, in_sem, z_send, z_recv, xy_send, xy_recv, swap_send, swap_recv, pass_send, pass_recv, home_send, home_recv,
    out_sem,
):
    grp, wide = lax.axis_index("grp"), lax.axis_index("wide")
    high, core = grp // 2, grp % 2
    low, place = wide // 16, wide % 16
    row, column = place // 4, place % 4
    plane = high * 2 + low

    def at(to_plane, to_place, to_core):
        return {"grp": (to_plane // 2) * 2 + to_core, "wide": (to_plane % 2) * 16 + to_place}

    def away(step):
        return (plane + step + 8) % 8

    def around(step):
        return ((row + step // 4) % 4) * 4 + (column + step % 4) % 4

    def await_all(ref, sem):
        pltpu.make_async_copy(ref, ref, sem).wait()

    loads = [
        pltpu.make_async_copy(echoes.at[:, pl.ds(n * 1024, 1024)], raw.at[:, pl.ds(n * 1024, 1024)], load_sem.at[n])
        for n in range(2)
    ]
    small = [
        pltpu.make_async_copy(a, b, in_sem.at[n])
        for n, (a, b) in enumerate([(choice, picks), (patterns, pats), (operator, oper)])
    ]
    for load in loads + small:
        load.start()

    barrier = pltpu.get_barrier_semaphore()

    def greet(device):
        pl.semaphore_signal(barrier, inc=1, device_id=device, device_id_type=MESH)

    for step in (-3, -2, -1, 1, 2, 3):
        greet(at(away(step), place, core))
    for step in range(1, 16):
        greet(at(plane, around(step), core))
    greet(at(plane, place, 1 - core))

    def turn(block, carry):
        slot = block % 2
        single[slot] = raw[:, pl.ds(pl.multiple_of(block * 64, 64), 64), :].astype(jnp.float32)
        for eighth in range(8):
            for chunk in range(CHUNKS):
                gate = eighth * 8 + chunk * 2
                both = jnp.concatenate([single[slot, :, gate], single[slot, :, gate + 1]], axis=0)
                turned[block % 16, block // 16, eighth, chunk] = both.astype(jnp.bfloat16)
        return carry

    for n in range(2):
        loads[n].wait()
        lax.fori_loop(n * 16, n * 16 + 16, turn, 0)
    pl.semaphore_wait(barrier, 22)

    for chunk in range(CHUNKS):
        for step in (3, -3, 2, -2, 1, -1):
            side = 0 if step > 0 else 1
            eighth = away(step) if step > 0 else away(step - 1)
            pltpu.make_async_remote_copy(
                src_ref=turned.at[:, :, eighth, chunk],
                dst_ref=mid.at[:, side, abs(step), :, chunk],
                send_sem=z_send.at[chunk],
                recv_sem=z_recv.at[chunk],
                device_id=at(away(step), place, core),
                device_id_type=MESH,
            ).start()
        for side in range(2):
            pltpu.make_async_copy(
                turned.at[:, :, away(-side), chunk], mid.at[:, side, 0, :, chunk], z_recv.at[chunk]
            ).start()

    def send_xy(chunk):
        await_all(mid.at[:, :, :, :, chunk], z_recv.at[chunk])

        def one(step, carry):
            to = around(step)
            pltpu.make_async_remote_copy(
                src_ref=mid.at[to, :, :, :, chunk],
                dst_ref=held.at[:, :, :, chunk, place],
                send_sem=xy_send.at[chunk],
                recv_sem=xy_recv.at[chunk],
                device_id=at(plane, to, core),
                device_id_type=MESH,
            ).start()
            return carry

        lax.fori_loop(1, 16, one, 0)
        pltpu.make_async_copy(
            mid.at[place, :, :, :, chunk], held.at[:, :, :, chunk, place], xy_recv.at[chunk]
        ).start()

    for load in small:
        load.wait()
    lane = lax.broadcasted_iota(jnp.int32, (512, 128), 1)
    number = lax.broadcasted_iota(jnp.int32, (256, 512), 0)
    for h in range(4):
        found = []
        for j in range(2):
            n = h * 4 + j
            pick = jnp.where(core == 0, picks[n : n + 1, :], picks[n + 2 : n + 3, :])
            hot = (pick == number).astype(jnp.float32).astype(jnp.bfloat16)
            found.append(jnp.dot(pats[...], hot, preferred_element_type=jnp.float32).T)
        real = jnp.where(lane < 64, found[0], pltpu.roll(found[1], 64, 1)).astype(jnp.bfloat16)
        imag = jnp.where(lane < 64, pltpu.roll(found[0], 64, 1), found[1]).astype(jnp.bfloat16)
        for beams in range(8):
            rows = slice(beams * 64, beams * 64 + 64)
            upper = slice((beams // 2) * 128, (beams // 2) * 128 + 64)
            lower = slice((beams // 2) * 128 + 64, (beams // 2) * 128 + 128)
            weights[beams % 2, h, upper, :128] = real[rows]
            weights[beams % 2, h, upper, 128:] = -imag[rows]
            weights[beams % 2, h, lower, :128] = imag[rows]
            weights[beams % 2, h, lower, 128:] = real[rows]

    def beams_of(owner, n):
        side = n // 2
        used = [weights[owner, away((2 * side - 1) * unit) // 2] for unit in range(4)]
        return lax.dot_general(
            jnp.concatenate(used, axis=1), dop[n], (((1,), (1,)), ((), ())), preferred_element_type=jnp.float32
        )

    def swap(chunk, n):
        return pltpu.make_async_remote_copy(
            src_ref=give.at[chunk, n],
            dst_ref=got.at[chunk, n],
            send_sem=swap_send.at[chunk, n],
            recv_sem=swap_recv.at[chunk, n],
            device_id=at(plane, place, 1 - core),
            device_id_type=MESH,
        )

    def hand(chunk, n):
        side, other = n // 2, n % 2
        to = (1 - side) * 2 + 1 - other
        return pltpu.make_async_remote_copy(
            src_ref=pass_on.at[chunk, n],
            dst_ref=passed.at[chunk, to],
            send_sem=pass_send.at[chunk, n],
            recv_sem=pass_recv.at[chunk, to],
            device_id=at(away(1 - 2 * side), place, core),
            device_id_type=MESH,
        )

    def partials(chunk):
        await_all(held.at[:, :, :, chunk], xy_recv.at[chunk])

        def first(n, carry):
            side, half = n // 2, (low + n) % 2
            samples = [held[side, unit, half, chunk].reshape(256, 128) for unit in range(4)]
            bins = []
            for odd in range(2):
                both = jnp.concatenate([samples[odd], samples[odd + 2]], axis=1)
                bins.append(
                    jnp.dot(oper[(low + odd) % 2], both, preferred_element_type=jnp.float32).astype(jnp.bfloat16)
                )
            parts = []
            for unit in range(4):
                of = bins[unit % 2][:, (unit // 2) * 128 : (unit // 2) * 128 + 128]
                parts += [of[:256], of[256:]]
            dop[n] = jnp.concatenate(parts, axis=1)
            give[chunk, n] = beams_of(1 - core, n).astype(jnp.bfloat16)
            swap(chunk, n).start()
            return carry

        def second(n, carry):
            mine[...] = beams_of(core, n).reshape(4, 128, 256)
            swap(chunk, n).wait()
            side, other = n // 2, n % 2
            ahead = 2 * side - 1
            for e in range(2):
                h = away(ahead * (other + 2 * e)) // 2
                keep[chunk, n, e] = mine[h] + got[chunk, n, pl.ds(pl.multiple_of(h * 128, 128), 128)].astype(jnp.float32)
                h = away(-ahead * (2 - other + 2 * e)) // 2
                both = mine[h] + got[chunk, n, pl.ds(pl.multiple_of(h * 128, 128), 128)].astype(jnp.float32)
                pass_on[chunk, n, e] = both.astype(jnp.bfloat16)
            hand(chunk, n).start()
            return carry

        lax.fori_loop(0, 4, first, 0)
        lax.fori_loop(0, 4, second, 0)

    def send_home(chunk):
        for n in range(4):
            side, other = n // 2, n % 2
            ahead = 2 * side - 1
            await_all(passed.at[chunk, n], pass_recv.at[chunk, n])
            for e in range(2):
                both = keep[chunk, n, e] + passed[chunk, n, e].astype(jnp.float32)
                done[chunk, n, e] = both.astype(jnp.bfloat16)
                far = other + 2 * e
                slot = 7 - far if side else far
                if far == 0:
                    pltpu.make_async_copy(
                        done.at[chunk, n, e], homed.at[slot, chunk], home_recv.at[slot, chunk]
                    ).start()
                else:
                    pltpu.make_async_remote_copy(
                        src_ref=done.at[chunk, n, e],
                        dst_ref=homed.at[slot, chunk],
                        send_sem=home_send,
                        recv_sem=home_recv.at[slot, chunk],
                        device_id=at(away(ahead * far), place, core),
                        device_id_type=MESH,
                    ).start()

    send_xy(0)

    def forward(chunk, carry):
        @pl.when(chunk < CHUNKS - 1)
        def _():
            send_xy(chunk + 1)

        @pl.when(chunk == CHUNKS - 1)
        def _():
            for earlier in range(CHUNKS - 1):
                send_home(earlier)

        partials(chunk)
        return carry

    lax.fori_loop(0, CHUNKS, forward, 0)
    send_home(CHUNKS - 1)

    for chunk in range(CHUNKS):

        def place_gates(eighth, carry):
            slot = (eighth - plane + 8) % 8
            await_all(homed.at[slot, chunk], home_recv.at[slot, chunk])
            for gate in range(2):
                piece = homed[slot, chunk, :, gate * 128 : gate * 128 + 128]
                spread[eighth, :, chunk * 2 + gate, :] = piece.astype(jnp.float32)
            return carry

        if chunk < CHUNKS - 1:
            lax.fori_loop(0, 8, place_gates, 0)
        else:
            for quarter in range(4):
                lax.fori_loop(quarter * 2, quarter * 2 + 2, place_gates, 0)
                rows = jnp.concatenate([spread[quarter * 2], spread[quarter * 2 + 1]], axis=1)
                final[quarter] = rows.astype(jnp.bfloat16)
                for part in range(2):
                    pltpu.make_async_copy(
                        final.at[quarter, pl.ds(part * 64, 64)],
                        out.at[:, part, pl.ds(quarter * 16, 16)],
                        out_sem,
                    ).start()

    for chunk in range(CHUNKS):
        await_all(turned.at[:, :, pl.ds(0, 6), chunk], z_send.at[chunk])
        await_all(mid.at[pl.ds(0, 15), :, :, :, chunk], xy_send.at[chunk])
        for n in range(4):
            await_all(pass_on.at[chunk, n], pass_send.at[chunk, n])
    await_all(homed.at[pl.ds(0, 6)], home_send)
    await_all(out, out_sem)


def shards(echoes, patterns, block_choice):
    bf16, f32 = jnp.bfloat16, jnp.float32
    anywhere = pl.BlockSpec(memory_space=pl.ANY)
    small = [
        patterns.transpose(1, 2, 0).reshape(128, 256),
        block_choice.T,
        jnp.asarray(doppler_operator(128, 32)),
    ]
    return pl.pallas_call(
        kernel,
        out_shape=jax.ShapeDtypeStruct((64, 2, 64, 128), bf16),
        in_specs=[anywhere] * 4,
        out_specs=anywhere,
        scratch_shapes=[
            pltpu.VMEM((8, 2048, 128), bf16),
            pltpu.VMEM((2, 8, 64, 128), f32),
            pltpu.VMEM((16, 2, 8, CHUNKS, 16, 128), bf16),
            pltpu.VMEM((16, 2, 4, 2, CHUNKS, 16, 128), bf16),
            pltpu.VMEM((2, 4, 2, CHUNKS, 16, 16, 128), bf16),
            pltpu.VMEM((2, 512, 256), bf16),
            pltpu.VMEM((128, 256), bf16),
            pltpu.VMEM((16, 512), jnp.int32),
            pltpu.VMEM((2, 4, 512, 256), bf16),
            pltpu.VMEM((4, 256, 1024), bf16),
            pltpu.VMEM((4, 128, 256), f32),
            pltpu.VMEM((CHUNKS, 4, 512, 256), bf16),
            pltpu.VMEM((CHUNKS, 4, 512, 256), bf16),
            pltpu.VMEM((CHUNKS, 4, 2, 128, 256), f32),
            pltpu.VMEM((CHUNKS, 4, 2, 128, 256), bf16),
            pltpu.VMEM((CHUNKS, 4, 2, 128, 256), bf16),
            pltpu.VMEM((CHUNKS, 4, 2, 128, 256), bf16),
            pltpu.VMEM((8, CHUNKS, 128, 256), bf16),
            pltpu.VMEM((8, 128, 8, 128), f32),
            pltpu.VMEM((4, 128, 16, 128), bf16),
            pltpu.SemaphoreType.DMA((2,)),
            pltpu.SemaphoreType.DMA((3,)),
            pltpu.SemaphoreType.DMA((CHUNKS,)),
            pltpu.SemaphoreType.DMA((CHUNKS,)),
            pltpu.SemaphoreType.DMA((CHUNKS,)),
            pltpu.SemaphoreType.DMA((CHUNKS,)),
            pltpu.SemaphoreType.DMA((CHUNKS, 4)),
            pltpu.SemaphoreType.DMA((CHUNKS, 4)),
            pltpu.SemaphoreType.DMA((CHUNKS, 4)),
            pltpu.SemaphoreType.DMA((CHUNKS, 4)),
            pltpu.SemaphoreType.DMA,
            pltpu.SemaphoreType.DMA((8, CHUNKS)),
            pltpu.SemaphoreType.DMA,
        ],
        compiler_params=pltpu.CompilerParams(
            collective_id=0, has_side_effects=True, vmem_limit_bytes=49 << 20
        ),
    )(
        echoes.reshape(8, 2048, 128),
        *[pltpu.with_memory_space_constraint(array, pltpu.HBM) for array in small],
    )


def solution(mesh):
    placed = (P(None, "wide", None, "grp"), P(), P())
    return jax.shard_map(
        shards, mesh=mesh, in_specs=placed, out_specs=P("grp", None, "wide", None), check_vma=False
    )
```

time: 275 us -> 142 us (0.52)
  blocking collectives: 163 us -> 0 us
  Pallas kernels: 0 us -> 140 us
  waiting for transfers between devices: 40.2 us -> 0 us
  local copies, waits for them, and re-layouts: 31 us -> 1.32 us
  matrix products: 20.5 us -> 0 us
  other arithmetic: 11.8 us -> 0 us
  starting transfers between devices: 7.73 us -> 0 us
    all_to_all x2 -> x0, blocking collectives: 163 us -> none  [the longest x1 105 us: shards(): lax.all_to_all(shaped, 'grp', split_axis=3, concat_axis=5, tiled=True)]
    pallas_call x0 -> x1, Pallas kernels: none -> 140 us  [shards(): pl.pallas_call(kernel, out_shape=jax.ShapeDtypeStruct((64, 2, 64, 128), b...]
    all_to_all x1 -> x0, waiting for transfers between devices: 40.2 us -> none  [shards(): lax.all_to_all(lax.all_to_all(shaped, 'grp', split_axis=3, concat_axis=5,...]
    dot_general x3 -> x0, matrix products: 20.5 us -> none  [the longest x1 10.6 us: form_beams(): jnp.einsum('boigc,gicnk->gbonk', grouped, doppler, preferred_element_type...]
    all_to_all x4 -> x0, local copies, waits for them, and re-layouts: 18.7 us -> none  [the longest x2 14.1 us: shards(): lax.all_to_all(shaped, 'grp', split_axis=3, concat_axis=5, tiled=True)]
    reduce_sum x1 -> x0, other arithmetic: 9.38 us -> none  [form_beams(): return jnp.sum(rounded, axis=0).astype(jnp.bfloat16)]
    all_to_all x1 -> x0, starting transfers between devices: 7.73 us -> none  [shards(): lax.all_to_all(lax.all_to_all(shaped, 'grp', split_axis=3, concat_axis=5,...]
    another operation x2 -> x0, local copies, waits for them, and re-layouts: 6.25 us -> none  [steering(): return jnp.stack([upper_rows, lower_rows], axis=1)]
  transfers between devices with their start and end apart: 1 -> 0, of which waited for: 1 -> 0; matrix products, arithmetic and copies ran while one was open for 4% -> 0% of each run, Pallas kernels for 0% -> 0%
where the time goes in v3:
time: 142 us; the launch traced here: 141 us
  Pallas kernels  140 us (99%)
    pallas_call x1, Pallas kernels, shards(): pl.pallas_call(kernel, out_shape=jax.ShapeDtypeStruct((64, 2, 64, 128), b...  140 us

profile of v3, /device:TPU:8, one launch (start us, length us, event | category | flops | bytes accessed | tf_op | source)
XLA Modules:
  0.0 141.1 jit_solution(5843797176605295255)
XLA Ops:
  0.0 139.8 %shard_map.46 = bf16[64,2,64,128]{3,2,1,0:T(8,128)(2,1)S(1)} custom-call(bf16[8,2048,128]{2,1,0:T(8,128)(2,1)} %bitcast.5, bf16[128,256]{1,0:T(8,128)(2,1)} %bitcast.6, s32[16,512]{1,0:T(8,128)} %bitcast.7, bf16[2,512,256]{2,1,0:T(8,128)(2,1)} %constant.2.clone.operator), custom_call_target="tpu_custom_call" | custom-call | tf_op jit(solution)/shard_map/pallas_call | solution.py:303
  139.8 1.3 copy.6

commit v4 on v3

--- a/solution.py
+++ b/solution.py
@@ -54,16 +54,16 @@
     def await_all(ref, sem):
         pltpu.make_async_copy(ref, ref, sem).wait()
 
+    quarters = [(high + step) % 4 for step in (1, 3, 2, 0)]
     loads = [
-        pltpu.make_async_copy(echoes.at[:, pl.ds(n * 1024, 1024)], raw.at[:, pl.ds(n * 1024, 1024)], load_sem.at[n])
-        for n in range(2)
+        pltpu.make_async_copy(echoes.at[:, :, quarter], raw.at[n], load_sem.at[n])
+        for n, quarter in enumerate(quarters)
     ]
     small = [
         pltpu.make_async_copy(a, b, in_sem.at[n])
         for n, (a, b) in enumerate([(choice, picks), (patterns, pats), (operator, oper)])
     ]
-    for load in loads + small:
-        load.start()
+    loads[0].start()
 
     barrier = pltpu.get_barrier_semaphore()
 
@@ -76,33 +76,51 @@
         greet(at(plane, around(step), core))
     greet(at(plane, place, 1 - core))
 
-    def turn(block, carry):
-        slot = block % 2
-        single[slot] = raw[:, pl.ds(pl.multiple_of(block * 64, 64), 64), :].astype(jnp.float32)
-        for eighth in range(8):
+    for load in loads[1:] + small:
+        load.start()
+
+    def turn(n, block):
+        slot = block % 4
+        single[slot] = raw[n, :, block].astype(jnp.float32)
+        for eighth in range(2):
             for chunk in range(CHUNKS):
                 gate = eighth * 8 + chunk * 2
                 both = jnp.concatenate([single[slot, :, gate], single[slot, :, gate + 1]], axis=0)
-                turned[block % 16, block // 16, eighth, chunk] = both.astype(jnp.bfloat16)
-        return carry
-
-    for n in range(2):
-        loads[n].wait()
-        lax.fori_loop(n * 16, n * 16 + 16, turn, 0)
-    pl.semaphore_wait(barrier, 22)
-
-    for chunk in range(CHUNKS):
-        for step in (3, -3, 2, -2, 1, -1):
-            side = 0 if step > 0 else 1
-            eighth = away(step) if step > 0 else away(step - 1)
+                turned[block % 16, block // 16, quarters[n] * 2 + eighth, chunk] = both.astype(jnp.bfloat16)
+
+    def send_z(eighth, chunk):
+        ahead = (eighth - plane + 8) % 8
+        side = ahead // 4
+        unit = ahead + side * (7 - 2 * ahead)
+
+        @pl.when(unit > 0)
+        def _():
             pltpu.make_async_remote_copy(
                 src_ref=turned.at[:, :, eighth, chunk],
-                dst_ref=mid.at[:, side, abs(step), :, chunk],
+                dst_ref=mid.at[:, side, unit, :, chunk],
                 send_sem=z_send.at[chunk],
                 recv_sem=z_recv.at[chunk],
-                device_id=at(away(step), place, core),
+                device_id=at(away(ahead - 7 * side), place, core),
                 device_id_type=MESH,
             ).start()
+
+    for n in range(4):
+        loads[n].wait()
+
+        def turn_some(some, carry):
+            for block in range(4):
+                turn(n, some * 4 + block)
+            return carry
+
+        lax.fori_loop(0, 8, turn_some, 0)
+        if n == 0:
+            pl.semaphore_wait(barrier, 22)
+        for eighth in range(2):
+            send_z(quarters[n] * 2 + eighth, 0)
+    for chunk in range(CHUNKS):
+        if chunk:
+            for step in (3, 4, 2, 5, 1, 6):
+                send_z(away(step), chunk)
         for side in range(2):
             pltpu.make_async_copy(
                 turned.at[:, :, away(-side), chunk], mid.at[:, side, 0, :, chunk], z_recv.at[chunk]
@@ -211,7 +229,11 @@
                 h = away(-ahead * (2 - other + 2 * e)) // 2
                 both = mine[h] + got[chunk, n, pl.ds(pl.multiple_of(h * 128, 128), 128)].astype(jnp.float32)
                 pass_on[chunk, n, e] = both.astype(jnp.bfloat16)
-            hand(chunk, n).start()
+
+            @pl.when(chunk > 0)
+            def _():
+                hand(chunk, n).start()
+
             return carry
 
         lax.fori_loop(0, 4, first, 0)
@@ -248,15 +270,21 @@
         def _():
             send_xy(chunk + 1)
 
+        @pl.when(chunk == CHUNKS - 2)
+        def _():
+            for n in range(4):
+                hand(0, n).start()
+
         @pl.when(chunk == CHUNKS - 1)
         def _():
-            for earlier in range(CHUNKS - 1):
+            for earlier in range(CHUNKS - 2):
                 send_home(earlier)
 
         partials(chunk)
         return carry
 
     lax.fori_loop(0, CHUNKS, forward, 0)
+    send_home(CHUNKS - 2)
     send_home(CHUNKS - 1)
 
     for chunk in range(CHUNKS):
@@ -306,8 +334,8 @@
         in_specs=[anywhere] * 4,
         out_specs=anywhere,
         scratch_shapes=[
-            pltpu.VMEM((8, 2048, 128), bf16),
-            pltpu.VMEM((2, 8, 64, 128), f32),
+            pltpu.VMEM((4, 8, 32, 16, 128), bf16),
+            pltpu.VMEM((4, 8, 16, 128), f32),
             pltpu.VMEM((16, 2, 8, CHUNKS, 16, 128), bf16),
             pltpu.VMEM((16, 2, 4, 2, CHUNKS, 16, 128), bf16),
             pltpu.VMEM((2, 4, 2, CHUNKS, 16, 16, 128), bf16),
@@ -326,7 +354,7 @@
             pltpu.VMEM((8, CHUNKS, 128, 256), bf16),
             pltpu.VMEM((8, 128, 8, 128), f32),
             pltpu.VMEM((4, 128, 16, 128), bf16),
-            pltpu.SemaphoreType.DMA((2,)),
+            pltpu.SemaphoreType.DMA((4,)),
             pltpu.SemaphoreType.DMA((3,)),
             pltpu.SemaphoreType.DMA((CHUNKS,)),
             pltpu.SemaphoreType.DMA((CHUNKS,)),
@@ -344,7 +372,7 @@
             collective_id=0, has_side_effects=True, vmem_limit_bytes=49 << 20
         ),
     )(
-        echoes.reshape(8, 2048, 128),
+        echoes.reshape(8, 32, 4, 16, 128),
         *[pltpu.with_memory_space_constraint(array, pltpu.HBM) for array in small],
     )
 

time: 142 us -> 140 us (0.986)
  Pallas kernels: 140 us -> 137 us
    pallas_call x1, Pallas kernels: 140 us -> 137 us  [shards(): pl.pallas_call(kernel, out_shape=jax.ShapeDtypeStruct((64, 2, 64, 128), b...]
where the time goes in v4:
time: 140 us; the launch traced here: 138 us
  Pallas kernels  137 us (98%)
    pallas_call x1, Pallas kernels, shards(): pl.pallas_call(kernel, out_shape=jax.ShapeDtypeStruct((64, 2, 64, 128), b...  137 us

profile of v4, /device:TPU:8, one launch (start us, length us, event | category | flops | bytes accessed | tf_op | source)
XLA Modules:
  0.0 137.9 jit_solution(18109081223800154569)
XLA Ops:
  0.0 136.6 %shard_map.46 = bf16[64,2,64,128]{3,2,1,0:T(8,128)(2,1)S(1)} custom-call(bf16[8,32,4,16,128]{4,3,2,1,0:T(8,128)(2,1)} %bitcast.5, bf16[128,256]{1,0:T(8,128)(2,1)} %bitcast.6, s32[16,512]{1,0:T(8,128)} %bitcast.7, bf16[2,512,256]{2,1,0:T(8,128)(2,1)} %constant.2.clone.operator), custom_call_target="tpu_custom_call" | custom-call | tf_op jit(solution)/shard_map/pallas_call | solution.py:331
  136.6 1.3 copy.6

commit v5 on v4

v5 whole, which is shorter than its diff:
```python
import math

import jax
import jax.numpy as jnp
import ml_dtypes
import numpy as np
from jax import lax
from jax.experimental import pallas as pl
from jax.experimental.pallas import tpu as pltpu
from jax.sharding import PartitionSpec as P

MESH = pl.DeviceIdType.MESH
CHUNKS = 4


def doppler_operator(length, wide):
    index = np.arange(length, dtype=np.int32)
    phases = index[:, None] * index[None, :] % length
    angles = phases.astype(np.float32) * np.float32(2.0 * math.pi / length)
    scale = np.float32(1.0 / math.sqrt(length))
    cosine = np.cos(angles) * scale
    sine = -np.sin(angles) * scale
    table = np.array([[cosine, -sine], [sine, cosine]], np.float32)
    table = table.transpose(0, 2, 1, 3).reshape(2, length, 2, wide, length // wide)
    full = np.zeros((2, 2, length, wide, 2, 2, length // wide), np.float32)
    for gate in range(2):
        full[:, gate, :, :, gate] = table.transpose(0, 1, 3, 2, 4)
    halves = full.reshape(4 * length, 2, 2 * length).transpose(1, 0, 2)
    return halves.astype(ml_dtypes.bfloat16)


def kernel(
    echoes, patterns, choice, operator, out,
    raw, single, turned, mid, held, oper, pats, picks, weights, dop, mine, give, got, keep, kept, to_middle, at_middle,
    back, passed, homed, spread,
    load_sem, in_sem, z_send, z_recv, xy_send, xy_recv, swap_send, swap_recv, middle_send, middle_recv, back_send,
    back_recv, home_send, home_recv, out_sem,
):
    grp, wide = lax.axis_index("grp"), lax.axis_index("wide")
    high, core = grp // 2, grp % 2
    low, place = wide // 16, wide % 16
    row, column = place // 4, place % 4
    plane = high * 2 + low

    def at(to_plane, to_place, to_core):
        return {"grp": (to_plane // 2) * 2 + to_core, "wide": (to_plane % 2) * 16 + to_place}

    def away(step):
        return (plane + step + 8) % 8

    def around(step):
        return ((row + step // 4) % 4) * 4 + (column + step % 4) % 4

    def await_all(ref, sem):
        pltpu.make_async_copy(ref, ref, sem).wait()

    quarters = [(high + step) % 4 for step in (1, 3, 2, 0)]
    loads = [
        pltpu.make_async_copy(echoes.at[:, quarter], raw.at[n], load_sem.at[n])
        for n, quarter in enumerate(quarters)
    ]
    small = [
        pltpu.make_async_copy(a, b, in_sem.at[n])
        for n, (a, b) in enumerate([(choice, picks), (patterns, pats), (operator, oper)])
    ]
    loads[0].start()

    barrier = pltpu.get_barrier_semaphore()

    def greet(device):
        pl.semaphore_signal(barrier, inc=1, device_id=device, device_id_type=MESH)

    for step in (-3, -2, -1, 1, 2, 3):
        greet(at(away(step), place, core))
    for step in range(1, 16):
        greet(at(plane, around(step), core))
    greet(at(plane, place, 1 - core))

    for load in loads[1:] + small:
        load.start()

    def turn(n, block):
        slot = block % 4
        for ip in range(8):
            single[slot, ip] = raw[n, ip * 32 + block].astype(jnp.float32)
        for eighth in range(2):
            for chunk in range(CHUNKS):
                gate = eighth * 8 + chunk * 2
                both = jnp.concatenate([single[slot, :, gate], single[slot, :, gate + 1]], axis=0)
                turned[block % 16, block // 16, quarters[n] * 2 + eighth, chunk] = both.astype(jnp.bfloat16)

    def send_z(eighth, chunk):
        ahead = (eighth - plane + 8) % 8
        side = ahead // 4
        unit = ahead + side * (7 - 2 * ahead)

        def to_worker(role):
            far = unit - role

            @pl.when(far > 0)
            def _():
                pltpu.make_async_remote_copy(
                    src_ref=turned.at[:, (low + far) % 2, eighth, chunk],
                    dst_ref=mid.at[:, side * 8 + role * 4 + far, chunk],
                    send_sem=z_send.at[chunk],
                    recv_sem=z_recv.at[chunk],
                    device_id=at(away((1 - 2 * side) * far), place, core),
                    device_id_type=MESH,
                ).start()

        to_worker(0)
        to_worker(1)

    def keep_z(chunk):
        for side in range(2):
            for slot, half, eighth in ((0, low, -side), (4, low, 1 - 3 * side), (7, 1 - low, -side)):
                pltpu.make_async_copy(
                    turned.at[:, half, away(eighth), chunk], mid.at[:, side * 8 + slot, chunk], z_recv.at[chunk]
                ).start()

    for n in range(4):
        loads[n].wait()

        def turn_some(some, carry):
            for block in range(4):
                turn(n, some * 4 + block)
            return carry

        lax.fori_loop(0, 8, turn_some, 0)
        if n == 0:
            pl.semaphore_wait(barrier, 22)
        for eighth in range(2):
            send_z(quarters[n] * 2 + eighth, 0)
    for chunk in range(CHUNKS):
        if chunk:
            for step in (3, 4, 2, 5, 1, 6):
                send_z(away(step), chunk)
        keep_z(chunk)

    def send_xy(chunk):
        await_all(mid.at[:, :, chunk], z_recv.at[chunk])

        def one(step, carry):
            to = around(step)
            pltpu.make_async_remote_copy(
                src_ref=mid.at[to, :, chunk],
                dst_ref=held.at[:, chunk, place],
                send_sem=xy_send.at[chunk],
                recv_sem=xy_recv.at[chunk],
                device_id=at(plane, to, core),
                device_id_type=MESH,
            ).start()
            return carry

        lax.fori_loop(1, 16, one, 0)
        pltpu.make_async_copy(mid.at[place, :, chunk], held.at[:, chunk, place], xy_recv.at[chunk]).start()

    for load in small:
        load.wait()
    lane = lax.broadcasted_iota(jnp.int32, (512, 128), 1)
    number = lax.broadcasted_iota(jnp.int32, (256, 512), 0)
    for h in range(4):
        found = []
        for j in range(2):
            n = h * 4 + j
            pick = jnp.where(core == 0, picks[n : n + 1, :], picks[n + 2 : n + 3, :])
            hot = (pick == number).astype(jnp.float32).astype(jnp.bfloat16)
            found.append(jnp.dot(pats[...], hot, preferred_element_type=jnp.float32).T)
        real = jnp.where(lane < 64, found[0], pltpu.roll(found[1], 64, 1)).astype(jnp.bfloat16)
        imag = jnp.where(lane < 64, pltpu.roll(found[0], 64, 1), found[1]).astype(jnp.bfloat16)
        for beams in range(8):
            rows = slice(beams * 64, beams * 64 + 64)
            upper = slice((beams // 2) * 128, (beams // 2) * 128 + 64)
            lower = slice((beams // 2) * 128 + 64, (beams // 2) * 128 + 128)
            weights[beams % 2, h, upper, :128] = real[rows]
            weights[beams % 2, h, upper, 128:] = -imag[rows]
            weights[beams % 2, h, lower, :128] = imag[rows]
            weights[beams % 2, h, lower, 128:] = real[rows]

    units = (4, 3, 1)

    def beams_of(owner, role, side):
        used = [weights[owner, away((2 * side - 1) * unit) // 2] for unit in range(units[role])]
        return lax.dot_general(
            jnp.concatenate(used, axis=1),
            dop[role, side, :, : units[role] * 256],
            (((1,), (1,)), ((), ())),
            preferred_element_type=jnp.float32,
        )

    def swap(chunk, role, side):
        return pltpu.make_async_remote_copy(
            src_ref=give.at[role, side],
            dst_ref=got.at[chunk % 2, role, side],
            send_sem=swap_send.at[chunk, role, side],
            recv_sem=swap_recv.at[chunk, role, side],
            device_id=at(plane, place, 1 - core),
            device_id_type=MESH,
        )

    def hand(chunk, role, side):
        to = (1 - side, side)[role]
        return pltpu.make_async_remote_copy(
            src_ref=to_middle.at[chunk, role, side],
            dst_ref=at_middle.at[chunk, role, to],
            send_sem=middle_send.at[chunk, role, side],
            recv_sem=middle_recv.at[chunk, role, to],
            device_id=at(away(1 - 2 * side), place, core),
            device_id_type=MESH,
        )

    def hand_back(chunk, role, side):
        to = (1 - side, side)[role]
        return pltpu.make_async_remote_copy(
            src_ref=back.at[chunk, role, side],
            dst_ref=passed.at[chunk, role, to],
            send_sem=back_send.at[chunk, role, side],
            recv_sem=back_recv.at[chunk, role, to],
            device_id=at(away((1 - 2 * side, 2 * side - 1)[role]), place, core),
            device_id_type=MESH,
        )

    def partials(chunk):
        await_all(held.at[:, chunk], xy_recv.at[chunk])

        def first(role, side):
            samples = [held[side * 8 + role * 4 - role // 2 + unit, chunk].reshape(256, 128) for unit in range(units[role])]
            bins = []
            for odd in range(min(units[role], 2)):
                both = jnp.concatenate(samples[odd::2], axis=1)
                bins.append(
                    jnp.dot(oper[(low + odd) % 2], both, preferred_element_type=jnp.float32).astype(jnp.bfloat16)
                )
            parts = []
            for unit in range(units[role]):
                of = bins[unit % 2][:, (unit // 2) * 128 : (unit // 2) * 128 + 128]
                parts += [of[:256], of[256:]]
            dop[role, side, :, : units[role] * 256] = jnp.concatenate(parts, axis=1)
            give[role, side] = beams_of(1 - core, role, side).astype(jnp.bfloat16)
            swap(chunk, role, side).start()

        def second(role, side):
            mine[...] = beams_of(core, role, side).reshape(4, 128, 256)
            swap(chunk, role, side).wait()
            ahead = 2 * side - 1

            def combined(step):
                h = away(step) // 2
                rows = pl.ds(pl.multiple_of(h * 128, 128), 128)
                return mine[h] + got[chunk % 2, role, side, rows].astype(jnp.float32)

            for e in range(2):
                if role == 2:
                    kept[chunk % 2, 0, side, e] = combined(-ahead * (1 + 2 * e))
                    kept[chunk % 2, 1, side, e] = combined(ahead * (1 + 2 * e))
                else:
                    keep[chunk, role, side, e] = combined(ahead * 2 * e)
                    to_middle[chunk, role, side, e] = combined(-ahead * (2 + 2 * e)).astype(jnp.bfloat16)
            if role < 2:
                hand(chunk, role, side).start()

        def both_sides(step, role):
            def one(side, carry):
                step(role, side)
                return carry

            lax.fori_loop(0, 2, one, 0)

        for step in (first, second):
            for role in range(3):
                both_sides(step, role)

    def add_middle(chunk):
        for role in range(2):
            for side in range(2):
                await_all(at_middle.at[chunk, 1 - role, side], middle_recv.at[chunk, 1 - role, side])
                for e in range(2):
                    both = kept[chunk % 2, role, side, e] + at_middle[chunk, 1 - role, side, e].astype(jnp.float32)
                    back[chunk, role, side, e] = both.astype(jnp.bfloat16)
                hand_back(chunk, role, side).start()

    def send_home(chunk):
        for role in range(2):
            for side in range(2):
                await_all(passed.at[chunk, role, side], back_recv.at[chunk, role, side])
                await_all(to_middle.at[chunk, role, side], middle_send.at[chunk, role, side])
                for e in (1, 0):
                    both = keep[chunk, role, side, e] + passed[chunk, role, side, e].astype(jnp.float32)
                    to_middle[chunk, role, side, e] = both.astype(jnp.bfloat16)
                    slot = 7 - role - 2 * e if side else role + 2 * e
                    if e == 0:
                        pltpu.make_async_copy(
                            to_middle.at[chunk, role, side, e], homed.at[slot, chunk], home_recv.at[slot, chunk]
                        ).start()
                    else:
                        pltpu.make_async_remote_copy(
                            src_ref=to_middle.at[chunk, role, side, e],
                            dst_ref=homed.at[slot, chunk],
                            send_sem=home_send,
                            recv_sem=home_recv.at[slot, chunk],
                            device_id=at(away((2 * side - 1) * 2), place, core),
                            device_id_type=MESH,
                        ).start()

    send_xy(0)

    def forward(chunk, carry):
        @pl.when(chunk < CHUNKS - 1)
        def _():
            send_xy(chunk + 1)

        @pl.when(chunk == CHUNKS - 2)
        def _():
            add_middle(0)

        @pl.when(chunk == CHUNKS - 1)
        def _():
            add_middle(1)
            send_home(0)

        partials(chunk)
        return carry

    lax.fori_loop(0, CHUNKS, forward, 0)
    add_middle(CHUNKS - 2)
    send_home(CHUNKS - 3)
    add_middle(CHUNKS - 1)
    send_home(CHUNKS - 2)
    send_home(CHUNKS - 1)

    for chunk in range(CHUNKS):

        def place_gates(eighth, carry):
            slot = (eighth - plane + 8) % 8
            await_all(homed.at[slot, chunk], home_recv.at[slot, chunk])
            for gate in range(2):
                piece = homed[slot, chunk, :, gate * 128 : gate * 128 + 128]
                spread[eighth, :, chunk * 2 + gate, :] = piece.astype(jnp.float32)
            return carry

        if chunk < CHUNKS - 1:
            lax.fori_loop(0, 8, place_gates, 0)
        else:
            for quarter in range(4):
                lax.fori_loop(quarter * 2, quarter * 2 + 2, place_gates, 0)
                rows = jnp.concatenate([spread[quarter * 2], spread[quarter * 2 + 1]], axis=1)
                raw[quarter, :128] = rows.astype(jnp.bfloat16)
                for part in range(2):
                    pltpu.make_async_copy(
                        raw.at[quarter, pl.ds(part * 64, 64)],
                        out.at[:, part, pl.ds(quarter * 16, 16)],
                        out_sem,
                    ).start()

    for chunk in range(CHUNKS):
        await_all(mid.at[:, pl.ds(0, 10), chunk], z_send.at[chunk])
        await_all(mid.at[pl.ds(0, 15), :, chunk], xy_send.at[chunk])
        for role in range(2):
            for side in range(2):
                await_all(back.at[chunk, role, side], back_send.at[chunk, role, side])
    await_all(homed.at[pl.ds(0, 4)], home_send)
    await_all(out, out_sem)


def shards(echoes, patterns, block_choice):
    bf16, f32 = jnp.bfloat16, jnp.float32
    anywhere = pl.BlockSpec(memory_space=pl.ANY)
    small = [
        patterns.transpose(1, 2, 0).reshape(128, 256),
        block_choice.T,
        jnp.asarray(doppler_operator(128, 32)),
    ]
    return pl.pallas_call(
        kernel,
        out_shape=jax.ShapeDtypeStruct((64, 2, 64, 128), bf16),
        in_specs=[anywhere] * 4,
        out_specs=anywhere,
        scratch_shapes=[
            pltpu.VMEM((4, 256, 16, 128), bf16),
            pltpu.VMEM((4, 8, 16, 128), f32),
            pltpu.VMEM((16, 2, 8, CHUNKS, 16, 128), bf16),
            pltpu.VMEM((16, 16, CHUNKS, 16, 128), bf16),
            pltpu.VMEM((16, CHUNKS, 16, 16, 128), bf16),
            pltpu.VMEM((2, 512, 256), bf16),
            pltpu.VMEM((128, 256), bf16),
            pltpu.VMEM((16, 512), jnp.int32),
            pltpu.VMEM((2, 4, 512, 256), bf16),
            pltpu.VMEM((3, 2, 256, 1024), bf16),
            pltpu.VMEM((4, 128, 256), f32),
            pltpu.VMEM((3, 2, 512, 256), bf16),
            pltpu.VMEM((2, 3, 2, 512, 256), bf16),
            pltpu.VMEM((CHUNKS, 2, 2, 2, 128, 256), f32),
            pltpu.VMEM((2, 2, 2, 2, 128, 256), f32),
            pltpu.VMEM((CHUNKS, 2, 2, 2, 128, 256), bf16),
            pltpu.VMEM((CHUNKS, 2, 2, 2, 128, 256), bf16),
            pltpu.VMEM((CHUNKS, 2, 2, 2, 128, 256), bf16),
            pltpu.VMEM((CHUNKS, 2, 2, 2, 128, 256), bf16),
            pltpu.VMEM((8, CHUNKS, 128, 256), bf16),
            pltpu.VMEM((8, 128, 8, 128), f32),
            pltpu.SemaphoreType.DMA((4,)),
            pltpu.SemaphoreType.DMA((3,)),
            pltpu.SemaphoreType.DMA((CHUNKS,)),
            pltpu.SemaphoreType.DMA((CHUNKS,)),
            pltpu.SemaphoreType.DMA((CHUNKS,)),
            pltpu.SemaphoreType.DMA((CHUNKS,)),
            pltpu.SemaphoreType.DMA((CHUNKS, 3, 2)),
            pltpu.SemaphoreType.DMA((CHUNKS, 3, 2)),
            pltpu.SemaphoreType.DMA((CHUNKS, 2, 2)),
            pltpu.SemaphoreType.DMA((CHUNKS, 2, 2)),
            pltpu.SemaphoreType.DMA((CHUNKS, 2, 2)),
            pltpu.SemaphoreType.DMA((CHUNKS, 2, 2)),
            pltpu.SemaphoreType.DMA,
            pltpu.SemaphoreType.DMA((8, CHUNKS)),
            pltpu.SemaphoreType.DMA,
        ],
        compiler_params=pltpu.CompilerParams(
            collective_id=0, has_side_effects=True, vmem_limit_bytes=50 << 20
        ),
    )(
        echoes.reshape(256, 4, 16, 128),
        *[pltpu.with_memory_space_constraint(array, pltpu.HBM) for array in small],
    )


def solution(mesh):
    placed = (P(None, "wide", None, "grp"), P(), P())
    return jax.shard_map(
        shards, mesh=mesh, in_specs=placed, out_specs=P("grp", None, "wide", None), check_vma=False
    )
```

time: 140 us -> 134 us (0.957)
  Pallas kernels: 137 us -> 132 us
    pallas_call x1, Pallas kernels: 137 us -> 132 us  [shards(): pl.pallas_call(kernel, out_shape=jax.ShapeDtypeStruct((64, 2, 64, 128), b...]
where the time goes in v5:
time: 134 us; the launch traced here: 133 us
  Pallas kernels  132 us (99%)
    pallas_call x1, Pallas kernels, shards(): pl.pallas_call(kernel, out_shape=jax.ShapeDtypeStruct((64, 2, 64, 128), b...  132 us

profile of v5, /device:TPU:8, one launch (start us, length us, event | category | flops | bytes accessed | tf_op | source)
XLA Modules:
  0.0 133.0 jit_solution(17231263131053605454)
XLA Ops:
  0.0 131.6 %shard_map.46 = bf16[64,2,64,128]{3,2,1,0:T(8,128)(2,1)S(1)} custom-call(bf16[256,4,16,128]{3,2,1,0:T(8,128)(2,1)} %bitcast.5, bf16[128,256]{1,0:T(8,128)(2,1)} %bitcast.6, s32[16,512]{1,0:T(8,128)} %bitcast.7, bf16[2,512,256]{2,1,0:T(8,128)(2,1)} %constant.2.clone.operator), custom_call_target="tpu_custom_call" | custom-call | tf_op jit(solution)/shard_map/pallas_call | solution.py:373
  131.6 1.3 copy.6

commit v6 on v4

v6 whole, which is shorter than its diff:
```python
import math

import jax
import jax.numpy as jnp
import ml_dtypes
import numpy as np
from jax import lax
from jax.experimental import pallas as pl
from jax.experimental.pallas import tpu as pltpu
from jax.sharding import PartitionSpec as P

MESH = pl.DeviceIdType.MESH
CHUNKS = 4


def doppler_operator(length, wide):
    index = np.arange(length, dtype=np.int32)
    phases = index[:, None] * index[None, :] % length
    angles = phases.astype(np.float32) * np.float32(2.0 * math.pi / length)
    scale = np.float32(1.0 / math.sqrt(length))
    cosine = np.cos(angles) * scale
    sine = -np.sin(angles) * scale
    table = np.array([[cosine, -sine], [sine, cosine]], np.float32)
    table = table.transpose(0, 2, 1, 3).reshape(2, length, 2, wide, length // wide)
    full = np.zeros((2, 2, length, wide, 2, 2, length // wide), np.float32)
    for gate in range(2):
        full[:, gate, :, :, gate] = table.transpose(0, 1, 3, 2, 4)
    return full.reshape(4 * length, 4 * length).T.reshape(2, 2 * length, 4 * length).astype(ml_dtypes.bfloat16)


def kernel(
    echoes, patterns, choice, operator, out,
    raw, single, turned, mid, held, oper, pats, picks, weights, mine, give, got, keep, pass_on, passed, keep_odd,
    pass_odd, passed_odd, to_mid, sums, near, far, home, home_odd, home_mid, spread,
    load_sem, in_sem, z_send, z_recv, xy_send, xy_recv, swap_send, swap_recv, pass_send, pass_recv, odd_send, odd_recv,
    mid_send, mid_recv, sums_send, sums_recv, near_send, near_recv, far_send, far_recv, out_sem,
):
    grp, wide = lax.axis_index("grp"), lax.axis_index("wide")
    high, core = grp // 2, grp % 2
    low, place = wide // 16, wide % 16
    row, column = place // 4, place % 4
    plane = high * 2 + low

    def at(to_plane, to_place, to_core):
        return {"grp": (to_plane // 2) * 2 + to_core, "wide": (to_plane % 2) * 16 + to_place}

    def away(step):
        return (plane + step + 8) % 8

    def around(step):
        return ((row + step // 4) % 4) * 4 + (column + step % 4) % 4

    def await_all(ref, sem):
        pltpu.make_async_copy(ref, ref, sem).wait()

    quarters = [(high + step) % 4 for step in (1, 2, 3, 0)]
    loads = [
        pltpu.make_async_copy(echoes.at[:, quarter], raw.at[n], load_sem.at[n])
        for n, quarter in enumerate(quarters)
    ]
    small = [
        pltpu.make_async_copy(a, b, in_sem.at[n])
        for n, (a, b) in enumerate([(choice, picks), (patterns, pats), (operator, oper)])
    ]
    loads[0].start()

    barrier = pltpu.get_barrier_semaphore()

    def greet(device):
        pl.semaphore_signal(barrier, inc=1, device_id=device, device_id_type=MESH)

    for step in (-3, -2, -1, 1, 2, 3):
        greet(at(away(step), place, core))
    for step in range(1, 16):
        greet(at(plane, around(step), core))
    greet(at(plane, place, 1 - core))

    for load in loads[1:] + small:
        load.start()

    def turn(n, block):
        slot = block % 4
        for ip in range(8):
            single[slot, ip] = raw[n, ip * 32 + block].astype(jnp.float32)
        for pair in range(8):
            both = jnp.concatenate([single[slot, :, pair * 2], single[slot, :, pair * 2 + 1]], axis=0)
            turned[block % 16, block // 16, quarters[n], pair] = both.astype(jnp.bfloat16)

    def of(chunk):
        return pl.ds(chunk * 2, 2)

    def send_z(chunk, side):
        pltpu.make_async_remote_copy(
            src_ref=turned.at[:, :, quarters[side], of(chunk)],
            dst_ref=mid.at[:, side, 1, :, of(chunk)],
            send_sem=z_send.at[chunk],
            recv_sem=z_recv.at[chunk],
            device_id=at(away(2 - 4 * side), place, core),
            device_id_type=MESH,
        ).start()

    for n in range(4):
        loads[n].wait()

        def turn_some(some, carry):
            for block in range(4):
                turn(n, some * 4 + block)
            return carry

        lax.fori_loop(0, 8, turn_some, 0)
        if n == 0:
            pl.semaphore_wait(barrier, 22)
        for chunk in range(CHUNKS):
            if n < 2:
                send_z(chunk, n)
            else:
                side = 3 - n
                pltpu.make_async_copy(
                    turned.at[:, :, quarters[n], of(chunk)], mid.at[:, side, 0, :, of(chunk)], z_recv.at[chunk]
                ).start()

    def send_xy(chunk):
        await_all(mid.at[:, :, :, :, of(chunk)], z_recv.at[chunk])

        def one(step, carry):
            to = around(step)
            pltpu.make_async_remote_copy(
                src_ref=mid.at[to, :, :, :, of(chunk)],
                dst_ref=held.at[:, :, :, of(chunk), place],
                send_sem=xy_send.at[chunk],
                recv_sem=xy_recv.at[chunk],
                device_id=at(plane, to, core),
                device_id_type=MESH,
            ).start()
            return carry

        lax.fori_loop(1, 16, one, 0)
        pltpu.make_async_copy(
            mid.at[place, :, :, :, of(chunk)], held.at[:, :, :, of(chunk), place], xy_recv.at[chunk]
        ).start()

    for load in small:
        load.wait()
    lane = lax.broadcasted_iota(jnp.int32, (512, 128), 1)
    number = lax.broadcasted_iota(jnp.int32, (256, 512), 0)
    for h in range(4):
        found = []
        for j in range(2):
            n = h * 4 + j
            pick = jnp.where(core == 0, picks[n : n + 1, :], picks[n + 2 : n + 3, :])
            hot = (pick == number).astype(jnp.float32).astype(jnp.bfloat16)
            found.append(jnp.dot(pats[...], hot, preferred_element_type=jnp.float32).T)
        real = jnp.where(lane < 64, found[0], pltpu.roll(found[1], 64, 1)).astype(jnp.bfloat16)
        imag = jnp.where(lane < 64, pltpu.roll(found[0], 64, 1), found[1]).astype(jnp.bfloat16)
        for beams in range(8):
            rows = slice(beams * 64, beams * 64 + 64)
            to = slice((beams // 2) * 64, (beams // 2) * 64 + 64)
            weights[beams % 2, h, 0, to] = real[rows]
            weights[beams % 2, h, 1, to] = imag[rows]

    real_lane = lax.broadcasted_iota(jnp.int32, (256, 256), 1) // 4 % 2 == 0

    def beams_of(owner, chunk, n):
        side, half, pair = n // 4, (low + n // 2) % 2, chunk * 2 + n % 2
        used = [weights[owner, h].reshape(512, 128) for h in (high, (high + 2 * side + 3) % 4)]
        samples = [held[side, unit, half, pair].reshape(256, 128) for unit in range(2)]
        both = lax.dot_general(
            jnp.concatenate(used, axis=1),
            jnp.concatenate(samples, axis=1),
            (((1,), (1,)), ((), ())),
            preferred_element_type=jnp.float32,
        )
        by_real, by_imag = both[:256], both[256:]
        return by_real + jnp.where(real_lane, -pltpu.roll(by_imag, 252, 1), pltpu.roll(by_imag, 4, 1))

    def remote(source, target, send, recv, step):
        return pltpu.make_async_remote_copy(
            src_ref=source,
            dst_ref=target,
            send_sem=send,
            recv_sem=recv,
            device_id=at(away(step), place, core),
            device_id_type=MESH,
        )

    def swap(chunk, n):
        return pltpu.make_async_remote_copy(
            src_ref=give.at[n],
            dst_ref=got.at[chunk % 2, n],
            send_sem=swap_send.at[chunk, n],
            recv_sem=swap_recv.at[chunk, n],
            device_id=at(plane, place, 1 - core),
            device_id_type=MESH,
        )

    def partials(chunk):
        await_all(held.at[:, :, :, of(chunk)], xy_recv.at[chunk])

        def first(n, carry):
            give[n] = beams_of(1 - core, chunk, n).astype(jnp.bfloat16)
            swap(chunk, n).start()
            return carry

        def second(side, carry):
            ahead = 2 * side - 1
            for other in range(2):
                for j in range(2):
                    n = side * 4 + other * 2 + j
                    mine[...] = beams_of(core, chunk, n).reshape(4, 64, 256)
                    swap(chunk, n).wait()

                    def combined(step):
                        h = away(step) // 2
                        rows = pl.ds(pl.multiple_of(h * 64, 64), 64)
                        return mine[h] + got[chunk % 2, n, rows].astype(jnp.float32)

                    if other == 0:
                        for e in range(2):
                            keep[chunk, side, j, e] = combined(ahead * 2 * e)
                            pass_on[chunk, side, j, e] = combined(-ahead * (2 + 2 * e)).astype(jnp.bfloat16)
                    else:
                        keep_odd[chunk, side, j] = combined(ahead)
                        pass_odd[chunk, side, j] = combined(-ahead * 3).astype(jnp.bfloat16)
                        to_mid[chunk, side, j] = combined(-ahead).astype(jnp.bfloat16)

                        @pl.when(side == j)
                        def _():
                            keep_odd[chunk, side, 2] = combined(ahead * 3)

                        @pl.when(side != j)
                        def _():
                            pass_odd[chunk, side, 2] = combined(ahead * 3).astype(jnp.bfloat16)

            remote(
                pass_on.at[chunk, side], passed.at[chunk, 1 - side],
                pass_send.at[chunk, side], pass_recv.at[chunk, 1 - side], -2 * ahead,
            ).start()
            remote(
                pass_odd.at[chunk, side], passed_odd.at[chunk, 1 - side],
                odd_send.at[chunk, side], odd_recv.at[chunk, 1 - side], -2 * ahead,
            ).start()
            remote(
                to_mid.at[chunk, side], home_mid.at[side, of(chunk)],
                mid_send.at[chunk, side], mid_recv.at[chunk, side], -ahead,
            ).start()
            return carry

        lax.fori_loop(0, 8, first, 0)
        lax.fori_loop(0, 2, second, 0)

    def combine(chunk):
        for side in range(2):
            ahead = 2 * side - 1
            await_all(passed_odd.at[chunk, side], odd_recv.at[chunk, side])
            both = keep_odd[chunk, side] + passed_odd[chunk, side].astype(jnp.float32)
            far[chunk, side] = both[2].astype(jnp.bfloat16)
            remote(
                far.at[chunk, side], home_odd.at[1, chunk * 2 + side],
                far_send.at[chunk, side], far_recv.at[chunk, side], 3 * ahead,
            ).start()
            near[chunk, side] = both[:2].astype(jnp.bfloat16)
            remote(
                near.at[chunk, side], home_odd.at[2 * side, of(chunk)],
                near_send.at[chunk, side], near_recv.at[chunk, side], ahead,
            ).start()
            await_all(passed.at[chunk, side], pass_recv.at[chunk, side])
            for j in range(2):
                both = keep[chunk, side, j] + passed[chunk, side, j].astype(jnp.float32)
                home[3 * side, chunk * 2 + j] = both[0].astype(jnp.bfloat16)
                sums[chunk, side, j] = both[1].astype(jnp.bfloat16)
            remote(
                sums.at[chunk, side], home.at[1 + side, of(chunk)],
                sums_send.at[chunk, side], sums_recv.at[chunk, side], 2 * ahead,
            ).start()

    send_xy(0)

    def forward(chunk, carry):
        @pl.when(chunk < CHUNKS - 1)
        def _():
            send_xy(chunk + 1)

        for late in range(2, CHUNKS):

            @pl.when(chunk == late)
            def _():
                combine(late - 2)

        partials(chunk)
        return carry

    lax.fori_loop(0, CHUNKS, forward, 0)
    combine(CHUNKS - 2)
    combine(CHUNKS - 1)

    for chunk in range(CHUNKS):
        for side in range(2):
            await_all(home_mid.at[side, of(chunk)], mid_recv.at[chunk, side])
            await_all(home_odd.at[2 * side, of(chunk)], near_recv.at[chunk, side])
            await_all(home_odd.at[1, chunk * 2 + side], far_recv.at[chunk, side])
        both = home_mid[0, of(chunk)].astype(jnp.float32) + home_mid[1, of(chunk)].astype(jnp.float32)
        home_odd[3, of(chunk)] = both.astype(jnp.bfloat16)
        for slot in (0, 3, 1, 2):
            if slot in (1, 2):
                await_all(home.at[slot, of(chunk)], sums_recv.at[chunk, slot - 1])
            quarter = (high + slot) % 4
            same = home[slot, of(chunk)].reshape(128, 256)
            others = home_odd[(slot + 4 - low) % 4, of(chunk)].reshape(128, 256)
            bins = jnp.dot(same, oper[low], preferred_element_type=jnp.float32)
            bins += jnp.dot(others, oper[1 - low], preferred_element_type=jnp.float32)
            for j in range(2):
                for o in range(2):
                    for gate in range(2):
                        piece = bins[j * 64 : j * 64 + 64, (o * 2 + gate) * 128 : (o * 2 + gate) * 128 + 128]
                        spread[quarter, o * 64 : o * 64 + 64, (chunk * 2 + j) * 2 + gate, :] = piece
            if chunk == CHUNKS - 1:
                raw[quarter, :128] = spread[quarter].astype(jnp.bfloat16)
                for o in range(2):
                    pltpu.make_async_copy(
                        raw.at[quarter, pl.ds(o * 64, 64)],
                        out.at[:, o, pl.ds(pl.multiple_of(quarter * 16, 16), 16)],
                        out_sem,
                    ).start()

    for chunk in range(CHUNKS):
        await_all(turned.at[:, :, pl.ds(0, 2), of(chunk)], z_send.at[chunk])
        await_all(mid.at[pl.ds(0, 15), :, :, :, of(chunk)], xy_send.at[chunk])
        for side in range(2):
            for ref, sem in (
                (pass_on, pass_send), (pass_odd, odd_send), (to_mid, mid_send), (sums, sums_send), (near, near_send),
                (far, far_send),
            ):
                await_all(ref.at[chunk, side], sem.at[chunk, side])
    await_all(out, out_sem)


def shards(echoes, patterns, block_choice):
    bf16, f32 = jnp.bfloat16, jnp.float32
    anywhere = pl.BlockSpec(memory_space=pl.ANY)
    small = [
        patterns.transpose(1, 2, 0).reshape(128, 256),
        block_choice.T,
        jnp.asarray(doppler_operator(128, 32)),
    ]
    return pl.pallas_call(
        kernel,
        out_shape=jax.ShapeDtypeStruct((64, 2, 64, 128), bf16),
        in_specs=[anywhere] * 4,
        out_specs=anywhere,
        scratch_shapes=[
            pltpu.VMEM((4, 256, 16, 128), bf16),
            pltpu.VMEM((4, 8, 16, 128), f32),
            pltpu.VMEM((16, 2, 4, 8, 16, 128), bf16),
            pltpu.VMEM((16, 2, 2, 2, 8, 16, 128), bf16),
            pltpu.VMEM((2, 2, 2, 8, 16, 16, 128), bf16),
            pltpu.VMEM((2, 256, 512), bf16),
            pltpu.VMEM((128, 256), bf16),
            pltpu.VMEM((16, 512), jnp.int32),
            pltpu.VMEM((2, 4, 2, 256, 128), bf16),
            pltpu.VMEM((4, 64, 256), f32),
            pltpu.VMEM((8, 256, 256), bf16),
            pltpu.VMEM((2, 8, 256, 256), bf16),
            pltpu.VMEM((CHUNKS, 2, 2, 2, 64, 256), f32),
            pltpu.VMEM((CHUNKS, 2, 2, 2, 64, 256), bf16),
            pltpu.VMEM((CHUNKS, 2, 2, 2, 64, 256), bf16),
            pltpu.VMEM((CHUNKS, 2, 3, 64, 256), f32),
            pltpu.VMEM((CHUNKS, 2, 3, 64, 256), bf16),
            pltpu.VMEM((CHUNKS, 2, 3, 64, 256), bf16),
            pltpu.VMEM((CHUNKS, 2, 2, 64, 256), bf16),
            pltpu.VMEM((CHUNKS, 2, 2, 64, 256), bf16),
            pltpu.VMEM((CHUNKS, 2, 2, 64, 256), bf16),
            pltpu.VMEM((CHUNKS, 2, 64, 256), bf16),
            pltpu.VMEM((4, 8, 64, 256), bf16),
            pltpu.VMEM((4, 8, 64, 256), bf16),
            pltpu.VMEM((2, 8, 64, 256), bf16),
            pltpu.VMEM((4, 128, 16, 128), f32),
            pltpu.SemaphoreType.DMA((4,)),
            pltpu.SemaphoreType.DMA((3,)),
            pltpu.SemaphoreType.DMA((CHUNKS,)),
            pltpu.SemaphoreType.DMA((CHUNKS,)),
            pltpu.SemaphoreType.DMA((CHUNKS,)),
            pltpu.SemaphoreType.DMA((CHUNKS,)),
            pltpu.SemaphoreType.DMA((CHUNKS, 8)),
            pltpu.SemaphoreType.DMA((CHUNKS, 8)),
        ]
        + [pltpu.SemaphoreType.DMA((CHUNKS, 2))] * 12
        + [pltpu.SemaphoreType.DMA],
        compiler_params=pltpu.CompilerParams(
            collective_id=0, has_side_effects=True, vmem_limit_bytes=50 << 20
        ),
    )(
        echoes.reshape(256, 4, 16, 128),
        *[pltpu.with_memory_space_constraint(array, pltpu.HBM) for array in small],
    )


def solution(mesh):
    placed = (P(None, "wide", None, "grp"), P(), P())
    return jax.shard_map(
        shards, mesh=mesh, in_specs=placed, out_specs=P("grp", None, "wide", None), check_vma=False
    )
```

time: 140 us -> 133 us (0.950)
  Pallas kernels: 137 us -> 129 us
    pallas_call x1, Pallas kernels: 137 us -> 129 us  [shards(): pl.pallas_call(kernel, out_shape=jax.ShapeDtypeStruct((64, 2, 64, 128), b...]
where the time goes in v6:
time: 133 us; the launch traced here: 130 us
  Pallas kernels  129 us (97%)
    pallas_call x1, Pallas kernels, shards(): pl.pallas_call(kernel, out_shape=jax.ShapeDtypeStruct((64, 2, 64, 128), b...  129 us

profile of v6, /device:TPU:8, one launch (start us, length us, event | category | flops | bytes accessed | tf_op | source)
XLA Modules:
  0.0 130.2 jit_solution(8743647618484165258)
XLA Ops:
  0.0 128.9 %shard_map.46 = bf16[64,2,64,128]{3,2,1,0:T(8,128)(2,1)S(1)} custom-call(bf16[256,4,16,128]{3,2,1,0:T(8,128)(2,1)} %bitcast.5, bf16[128,256]{1,0:T(8,128)(2,1)} %bitcast.6, s32[16,512]{1,0:T(8,128)} %bitcast.7, bf16[2,256,512]{2,1,0:T(8,128)(2,1)} %constant.2.clone.operator), custom_call_target="tpu_custom_call" | custom-call | tf_op jit(solution)/shard_map/pallas_call | solution.py:345
  128.9 1.3 %copy.6 = bf16[64,2,64,128]{3,2,1,0:T(8,128)(2,1)} copy(bf16[64,2,64,128]{3,2,1,0:T(8,128)(2,1)S(1)} %shard_map.46) | data formatting | bytes 4194304

commit v7 on v6

--- a/solution.py
+++ b/solution.py
@@ -31,7 +31,7 @@
 def kernel(
     echoes, patterns, choice, operator, out,
     raw, single, turned, mid, held, oper, pats, picks, weights, mine, give, got, keep, pass_on, passed, keep_odd,
-    pass_odd, passed_odd, to_mid, sums, near, far, home, home_odd, home_mid, spread,
+    pass_odd, passed_odd, to_mid, sums, near, far, home, home_odd, home_mid, spread, odd_bins,
     load_sem, in_sem, z_send, z_recv, xy_send, xy_recv, swap_send, swap_recv, pass_send, pass_recv, odd_send, odd_recv,
     mid_send, mid_recv, sums_send, sums_recv, near_send, near_recv, far_send, far_recv, out_sem,
 ):
@@ -112,7 +112,8 @@
             pl.semaphore_wait(barrier, 22)
         for chunk in range(CHUNKS):
             if n < 2:
-                send_z(chunk, n)
+                if chunk < 2:
+                    send_z(chunk, n)
             else:
                 side = 3 - n
                 pltpu.make_async_copy(
@@ -121,6 +122,11 @@
 
     def send_xy(chunk):
         await_all(mid.at[:, :, :, :, of(chunk)], z_recv.at[chunk])
+
+        @pl.when(chunk < CHUNKS - 2)
+        def _():
+            for side in range(2):
+                send_z(chunk + 2, side)
 
         def one(step, carry):
             to = around(step)
@@ -300,14 +306,20 @@
             await_all(home_odd.at[1, chunk * 2 + side], far_recv.at[chunk, side])
         both = home_mid[0, of(chunk)].astype(jnp.float32) + home_mid[1, of(chunk)].astype(jnp.float32)
         home_odd[3, of(chunk)] = both.astype(jnp.bfloat16)
+        for slot in (1, 2):
+            others = home_odd[(slot + 4 - low) % 4, of(chunk)].reshape(128, 256)
+            odd_bins[slot - 1] = jnp.dot(others, oper[1 - low], preferred_element_type=jnp.float32)
         for slot in (0, 3, 1, 2):
+            quarter = (high + slot) % 4
             if slot in (1, 2):
                 await_all(home.at[slot, of(chunk)], sums_recv.at[chunk, slot - 1])
-            quarter = (high + slot) % 4
             same = home[slot, of(chunk)].reshape(128, 256)
-            others = home_odd[(slot + 4 - low) % 4, of(chunk)].reshape(128, 256)
             bins = jnp.dot(same, oper[low], preferred_element_type=jnp.float32)
-            bins += jnp.dot(others, oper[1 - low], preferred_element_type=jnp.float32)
+            if slot in (1, 2):
+                bins += odd_bins[slot - 1]
+            else:
+                others = home_odd[(slot + 4 - low) % 4, of(chunk)].reshape(128, 256)
+                bins += jnp.dot(others, oper[1 - low], preferred_element_type=jnp.float32)
             for j in range(2):
                 for o in range(2):
                     for gate in range(2):
@@ -374,6 +386,7 @@
             pltpu.VMEM((4, 8, 64, 256), bf16),
             pltpu.VMEM((2, 8, 64, 256), bf16),
             pltpu.VMEM((4, 128, 16, 128), f32),
+            pltpu.VMEM((2, 128, 512), f32),
             pltpu.SemaphoreType.DMA((4,)),
             pltpu.SemaphoreType.DMA((3,)),
             pltpu.SemaphoreType.DMA((CHUNKS,)),

time: 133 us -> 132 us (level)
  no operation moved by 1% of the time
where the time goes in v7:
time: 132 us; the launch traced here: 130 us
  Pallas kernels  129 us (98%)
  local copies, waits for them, and re-layouts  1.32 us (1%)
    pallas_call x1, Pallas kernels, shards(): pl.pallas_call(kernel, out_shape=jax.ShapeDtypeStruct((64, 2, 64, 128), b...  129 us

profile of v7, /device:TPU:8, one launch (start us, length us, event | category | flops | bytes accessed | tf_op | source)
XLA Modules:
  0.0 130.3 jit_solution(6379412870357403705)
XLA Ops:
  0.0 129.0 %shard_map.46 = bf16[64,2,64,128]{3,2,1,0:T(8,128)(2,1)S(1)} custom-call(bf16[256,4,16,128]{3,2,1,0:T(8,128)(2,1)} %bitcast.5, bf16[128,256]{1,0:T(8,128)(2,1)} %bitcast.6, s32[16,512]{1,0:T(8,128)} %bitcast.7, bf16[2,256,512]{2,1,0:T(8,128)(2,1)} %constant.2.clone.operator), custom_call_target="tpu_custom_call" | custom-call | tf_op jit(solution)/shard_map/pallas_call | solution.py:357
  129.0 1.3 %copy.6 = bf16[64,2,64,128]{3,2,1,0:T(8,128)(2,1)} copy(bf16[64,2,64,128]{3,2,1,0:T(8,128)(2,1)S(1)} %shard_map.46) | data formatting | bytes 4194304

commit v8 on v7

--- a/solution.py
+++ b/solution.py
@@ -48,6 +48,7 @@
         return (plane + step + 8) % 8
 
     def around(step):
+        step = step * 7 % 16
         return ((row + step // 4) % 4) * 4 + (column + step % 4) % 4
 
     def await_all(ref, sem):

time: 132 us -> 132 us (level); the launches traced: 130 us -> 132 us
  Pallas kernels: 129 us -> 131 us
    pallas_call x1, Pallas kernels: 129 us -> 131 us  [shards(): pl.pallas_call(kernel, out_shape=jax.ShapeDtypeStruct((64, 2, 64, 128), b...]
where the time goes in v8:
time: 132 us
  Pallas kernels  131 us (99%)
  local copies, waits for them, and re-layouts  1.32 us (1%)
    pallas_call x1, Pallas kernels, shards(): pl.pallas_call(kernel, out_shape=jax.ShapeDtypeStruct((64, 2, 64, 128), b...  131 us

profile of v8, /device:TPU:8, one launch (start us, length us, event | category | flops | bytes accessed | tf_op | source)
XLA Modules:
  0.0 131.9 jit_solution(18130178257753524125)
XLA Ops:
  0.0 130.6 %shard_map.46 = bf16[64,2,64,128]{3,2,1,0:T(8,128)(2,1)S(1)} custom-call(bf16[256,4,16,128]{3,2,1,0:T(8,128)(2,1)} %bitcast.5, bf16[128,256]{1,0:T(8,128)(2,1)} %bitcast.6, s32[16,512]{1,0:T(8,128)} %bitcast.7, bf16[2,256,512]{2,1,0:T(8,128)(2,1)} %constant.2.clone.operator), custom_call_target="tpu_custom_call" | custom-call | tf_op jit(solution)/shard_map/pallas_call | solution.py:358
  130.6 1.3 %copy.6 = bf16[64,2,64,128]{3,2,1,0:T(8,128)(2,1)} copy(bf16[64,2,64,128]{3,2,1,0:T(8,128)(2,1)S(1)} %shard_map.46) | data formatting | bytes 4194304
